TPU v7x, 128 devices: a whole 4x4x4 slice. The times are simulated.
128 devices in a mesh: ctx: 32 (over z, x, core), head: 4 (over y).
Axes of the slice: x: 4, y: 4, z: 4, core: 2. Of those that a mesh axis runs over, the one named last changes fastest.
Arguments:
- queries: float32 [32768, 8, 256], P('ctx', 'head'), may hold values from -6 to 6
- keys: float32 [32768, 8, 256], P('ctx', 'head'), may hold values from -6 to 6
- values: float32 [32768, 8, 512], P('ctx', 'head'), may hold values from -6 to 6
- entry_gate_logit: float32 [8, 32768], P('head', 'ctx'), may hold values from -10 to 300
- forget_gate: float32 [8, 32768], P('head', 'ctx'), may hold values from 0 to 20
- out_weight: bfloat16 [4096, 4096], P('head'), may hold values from -0.09375 to 0.09375
Outputs:
- mixed: bfloat16 [32768, 4096], P('ctx', 'head')
All inputs are finite; a program needn't handle non-finite values.
Results may differ from a plain program's by a relative error of at most 0.013.
Values may be sent and summed in bfloat16 or wider, within the bound.
A program may use at most 192 MiB of HBM per device.

v0:
```python
import jax
import jax.numpy as jnp
from jax import lax
from jax.sharding import PartitionSpec as P


def passed_along(block, axis, distance):
    devices = range(lax.axis_size(axis))
    route = [(i - distance, i) for i in devices if i - distance in devices]
    return lax.ppermute(block, axis, route)


def block_pass(carry, pieces):
    state_c, state_n, state_m = carry
    q_rows, k_rows, v_rows, gate_in, gate_log = pieces
    size = gate_log.shape[0]
    scale_factor = q_rows.shape[1] ** (-0.5)
    cum = jnp.cumsum(gate_log)
    logits = cum[:, None] - cum[None, :] + gate_in[None, :]
    lower = jnp.tril(jnp.ones((size, size), dtype=bool))
    logits = jnp.where(lower, logits, -jnp.inf)
    carried = cum + state_m
    top = jnp.maximum(jnp.max(logits, axis=1), carried)
    decays = jnp.exp(logits - top[:, None])
    scores = jnp.dot(q_rows, k_rows.T, precision=lax.Precision.HIGHEST) * scale_factor
    weights = decays * scores
    carry_w = jnp.exp(carried - top)
    num = jnp.dot(weights, v_rows, precision=lax.Precision.HIGHEST)
    num = (
        num
        + carry_w[:, None]
        * jnp.dot(q_rows, state_c, precision=lax.Precision.HIGHEST)
        * scale_factor
    )
    den = (
        jnp.sum(weights, axis=1)
        + carry_w * jnp.dot(q_rows, state_n, precision=lax.Precision.HIGHEST) * scale_factor
    )
    last = cum[-1]
    keep = last - cum + gate_in
    new_m = jnp.maximum(last + state_m, jnp.max(keep))
    retained_entries = jnp.exp(keep - new_m)[:, None] * k_rows
    old_w = jnp.exp(last + state_m - new_m)
    new_c = old_w * state_c + jnp.dot(retained_entries.T, v_rows, precision=lax.Precision.HIGHEST)
    new_n = old_w * state_n + jnp.sum(retained_entries, axis=0)
    return ((new_c, new_n, new_m), (num, den, top))


def combine(earlier, later):
    sum_a, top_a, mem_a, norm_a = earlier
    sum_b, top_b, mem_b, norm_b = later
    top = jnp.maximum(sum_b + top_a, top_b)
    weight_a = jnp.exp(sum_b + top_a - top)
    weight_b = jnp.exp(top_b - top)
    memory = weight_a[:, None, None] * mem_a + weight_b[:, None, None] * mem_b
    denominator_vector = weight_a[:, None] * norm_a + weight_b[:, None] * norm_b
    return (sum_a + sum_b, top, memory, denominator_vector)


def on_device(queries, keys, values, entry_gate_logit, forget_gate, out_weight):
    rows, heads, width_k = queries.shape
    width_v = values.shape[2]
    block = min(512, rows)
    count = rows // block
    gate_log = jax.nn.log_sigmoid(forget_gate)

    def one_head(q_all, k_all, v_all, gate_in, log_all):
        blocks = (
            q_all.reshape(count, block, width_k),
            k_all.reshape(count, block, width_k),
            v_all.reshape(count, block, width_v),
            gate_in.reshape(count, block),
            log_all.reshape(count, block),
        )
        start = (
            jnp.zeros((width_k, width_v), jnp.float32),
            jnp.zeros((width_k,), jnp.float32),
            jnp.full((), -1e30, jnp.float32),
        )
        final, outputs = lax.scan(block_pass, start, blocks)
        num = outputs[0].reshape(rows, width_v)
        den = outputs[1].reshape(rows)
        top = outputs[2].reshape(rows)
        return (final, num, den, top, jnp.cumsum(log_all))

    final, num, den, top, cum = jax.vmap(one_head, in_axes=(1, 1, 1, 0, 0))(
        queries, keys, values, entry_gate_logit, gate_log
    )
    own = (jnp.sum(gate_log, axis=1), final[2], final[0], final[1])
    identity = (
        jnp.zeros((heads,), jnp.float32),
        jnp.full((heads,), -1e30, jnp.float32),
        jnp.zeros((heads, width_k, width_v), jnp.float32),
        jnp.zeros((heads, width_k), jnp.float32),
    )
    leading = lax.axis_index("ctx") == 0

    def relay(step, running):
        arrived = passed_along(combine(running, own), "ctx", 1)
        return jax.tree.map(lambda got, base: jnp.where(leading, base, got), arrived, identity)

    prefix_state = lax.fori_loop(0, lax.axis_size("ctx") - 1, relay, identity)
    scale_factor = width_k ** (-0.5)
    carried = cum + prefix_state[1][:, None]
    top_all = jnp.maximum(top, carried)
    own_w = jnp.exp(top - top_all)
    in_w = jnp.exp(carried - top_all)
    from_memory = (
        jnp.einsum("ifj,fjp->fip", queries, prefix_state[2], precision=lax.Precision.HIGHEST)
        * scale_factor
    )
    from_normer = (
        jnp.einsum("thk,hk->ht", queries, prefix_state[3], precision=lax.Precision.HIGHEST)
        * scale_factor
    )
    num_all = own_w[:, :, None] * num + in_w[:, :, None] * from_memory
    den_all = own_w * den + in_w * from_normer
    hidden = (num_all / jnp.maximum(jnp.abs(den_all), 1.0)[:, :, None]).astype(jnp.bfloat16)
    weight_heads = out_weight.reshape(heads, width_v, out_weight.shape[1])
    terms = jnp.einsum("htv,hvd->td", hidden, weight_heads, preferred_element_type=jnp.float32)
    return lax.psum_scatter(terms.astype(jnp.bfloat16), "head", scatter_dimension=1, tiled=True)


def solution(mesh):
    placed = (
        P("ctx", "head", None),
        P("ctx", "head", None),
        P("ctx", "head", None),
        P("head", "ctx"),
        P("head", "ctx"),
        P("head", None),
    )
    return jax.shard_map(
        on_device, mesh=mesh, in_specs=placed, out_specs=P("ctx", "head"), check_vma=False
    )
```

profile of v0, /device:TPU:1, one launch (start us, length us, event | category | flops | bytes accessed | tf_op | source)
XLA Modules:
  0.0 823.3 jit_solution(11268674871376067129)
XLA Ops:
  14.9 51.1 %while.36 = (s32[]{:T(128)}, f32[2,256,512]{2,1,0:T(8,128)S(1)}, f32[2,256]{1,0:T(2,128)S(1)}, f32[2]{0:T(128)S(1)}, f32[2,2,512,512]{3,2,0,1:T(8,128)}, /*index...) while((s32[]{:T(128)}, f32[2,256,512]{2,1,0:T(8,128)S(1)}, ...), condition=%wide.region_7.8_spmd.clone, body=%wide.region_0.7_spmd.clone.sunk | while | flops 8065790976 | bytes 50266184 | solution.py:80
  29.9 7.2 add_bitcast_fusion.3
  55.5 7.2 add_bitcast_fusion.3
  67.0 626.2 %while.37 = (s32[]{:T(128)}, f32[2]{0:T(128)S(1)}, f32[2,256,512]{2,1,0:T(8,128)}, f32[2,256]{1,0:T(2,128)S(1)}, pred[]{:T(512)}, /*index=5*/f32[2]{0:T(128)S(1)...) while((s32[]{:T(128)}, f32[2]{0:T(128)S(1)}, ...), condition=%wide.region_12.13_spmd.clone, body=%wide.region_11.12_spmd.clone.sunk | while | flops 1313295 | bytes 9456004 | solution.py:102
  255.8 6.5 collective-permute-start.1
  276.7 6.5 collective-permute-start.1
  297.6 6.5 collective-permute-start.1
  318.5 6.5 collective-permute-start.1
  339.4 6.5 collective-permute-start.1
  360.3 6.5 collective-permute-start.1
  381.2 6.5 collective-permute-start.1
  402.1 6.5 collective-permute-start.1
  423.0 6.5 collective-permute-start.1
  443.9 6.5 collective-permute-start.1
  464.8 6.5 collective-permute-start.1
  485.7 6.5 collective-permute-start.1
  506.6 6.5 collective-permute-start.1
  527.5 6.5 collective-permute-start.1
  548.4 6.5 collective-permute-start.1
  569.4 6.5 collective-permute-start.1
  632.1 6.5 collective-permute-start.1
  653.0 6.5 collective-permute-start.1
  703.5 10.8 %bitcast_convert_fusion = bf16[1024,4096]{1,0:T(8,128)(2,1)} fusion(bf16[2,1024,512]{2,1,0:T(8,128)(2,1)S(1)} %fusion.45, bf16[2,512,4096]{2,1,0:T(8,128)(2,1)S(1)} %bitcast.191), kind=kOutput, calls=%fused_computation.70 | convolution fusion | flops 8594128896 | bytes 18874368 | tf_op jit(solution)/shard_map/htv,hvd->td/dot_general | solution.py:120
  714.3 102.1 %reduce-scatter.2.cloned.1.call-done = bf16[1024,1024]{1,0:T(8,128)(2,1)} async-done(((bf16[1024,4096]{1,0:T(8,128)(2,1)}), bf16[1024,1024]{1,0:T(8,128)(2,1)}) %reduce-scatter.2.cloned.1.call-update) | async-done | bytes 2097168 | tf_op jit(solution)/shard_map/reduce_scatter | solution.py:121
  (481 shorter events, 563.8 us)
Async XLA Ops:
  6.5 809.9 %reduce-scatter.2.cloned.1.call-start = ((), (), s32[]{:S(2)}) async-start(), calls=%async_computation.1 | async-start | bytes 10485760 | tf_op jit(solution)/shard_map/reduce_scatter | solution.py:121
  67.3 16.3 %collective-permute-start.1 = (f32[2,256,512]{2,1,0:T(8,128)S(1)}, f32[2,256,512]{2,1,0:T(8,128)S(1)}, u32[]{:S(2)}, u32[]{:S(2)}) collective-permute-start(f32[2,256,512]{2,1,0:T(8,128)S(1)} %fusion.104), channel_id=1, source_target_pairs={{0,4},{4,8},{8,12},{12,16},{16,20},{20,24},{24,28},{28,32},{32,36}... | collective-permute-start | bytes 3145736 | tf_op jit(solution)/shard_map/while/body/eval_jaxpr/ppermute | solution.py:10
  236.6 16.6 %collective-permute-start.1 = (f32[2,256,512]{2,1,0:T(8,128)S(1)}, f32[2,256,512]{2,1,0:T(8,128)S(1)}, u32[]{:S(2)}, u32[]{:S(2)}) collective-permute-start(f32[2,256,512]{2,1,0:T(8,128)S(1)} %fusion.104), channel_id=1, source_target_pairs={{0,4},{4,8},{8,12},{12,16},{16,20},{20,24},{24,28},{28,32},{32,36}... | collective-permute-start | bytes 3145736 | tf_op jit(solution)/shard_map/while/body/eval_jaxpr/ppermute | solution.py:10
  255.8 18.3 %collective-permute-start.1 = (f32[2,256,512]{2,1,0:T(8,128)S(1)}, f32[2,256,512]{2,1,0:T(8,128)S(1)}, u32[]{:S(2)}, u32[]{:S(2)}) collective-permute-start(f32[2,256,512]{2,1,0:T(8,128)S(1)} %fusion.104), channel_id=1, source_target_pairs={{0,4},{4,8},{8,12},{12,16},{16,20},{20,24},{24,28},{28,32},{32,36}... | collective-permute-start | bytes 3145736 | tf_op jit(solution)/shard_map/while/body/eval_jaxpr/ppermute | solution.py:10
  276.7 18.3 %collective-permute-start.1 = (f32[2,256,512]{2,1,0:T(8,128)S(1)}, f32[2,256,512]{2,1,0:T(8,128)S(1)}, u32[]{:S(2)}, u32[]{:S(2)}) collective-permute-start(f32[2,256,512]{2,1,0:T(8,128)S(1)} %fusion.104), channel_id=1, source_target_pairs={{0,4},{4,8},{8,12},{12,16},{16,20},{20,24},{24,28},{28,32},{32,36}... | collective-permute-start | bytes 3145736 | tf_op jit(solution)/shard_map/while/body/eval_jaxpr/ppermute | solution.py:10
  297.6 18.3 %collective-permute-start.1 = (f32[2,256,512]{2,1,0:T(8,128)S(1)}, f32[2,256,512]{2,1,0:T(8,128)S(1)}, u32[]{:S(2)}, u32[]{:S(2)}) collective-permute-start(f32[2,256,512]{2,1,0:T(8,128)S(1)} %fusion.104), channel_id=1, source_target_pairs={{0,4},{4,8},{8,12},{12,16},{16,20},{20,24},{24,28},{28,32},{32,36}... | collective-permute-start | bytes 3145736 | tf_op jit(solution)/shard_map/while/body/eval_jaxpr/ppermute | solution.py:10
  318.5 18.3 %collective-permute-start.1 = (f32[2,256,512]{2,1,0:T(8,128)S(1)}, f32[2,256,512]{2,1,0:T(8,128)S(1)}, u32[]{:S(2)}, u32[]{:S(2)}) collective-permute-start(f32[2,256,512]{2,1,0:T(8,128)S(1)} %fusion.104), channel_id=1, source_target_pairs={{0,4},{4,8},{8,12},{12,16},{16,20},{20,24},{24,28},{28,32},{32,36}... | collective-permute-start | bytes 3145736 | tf_op jit(solution)/shard_map/while/body/eval_jaxpr/ppermute | solution.py:10
  339.4 18.3 %collective-permute-start.1 = (f32[2,256,512]{2,1,0:T(8,128)S(1)}, f32[2,256,512]{2,1,0:T(8,128)S(1)}, u32[]{:S(2)}, u32[]{:S(2)}) collective-permute-start(f32[2,256,512]{2,1,0:T(8,128)S(1)} %fusion.104), channel_id=1, source_target_pairs={{0,4},{4,8},{8,12},{12,16},{16,20},{20,24},{24,28},{28,32},{32,36}... | collective-permute-start | bytes 3145736 | tf_op jit(solution)/shard_map/while/body/eval_jaxpr/ppermute | solution.py:10
  360.3 18.3 %collective-permute-start.1 = (f32[2,256,512]{2,1,0:T(8,128)S(1)}, f32[2,256,512]{2,1,0:T(8,128)S(1)}, u32[]{:S(2)}, u32[]{:S(2)}) collective-permute-start(f32[2,256,512]{2,1,0:T(8,128)S(1)} %fusion.104), channel_id=1, source_target_pairs={{0,4},{4,8},{8,12},{12,16},{16,20},{20,24},{24,28},{28,32},{32,36}... | collective-permute-start | bytes 3145736 | tf_op jit(solution)/shard_map/while/body/eval_jaxpr/ppermute | solution.py:10
  381.2 18.3 %collective-permute-start.1 = (f32[2,256,512]{2,1,0:T(8,128)S(1)}, f32[2,256,512]{2,1,0:T(8,128)S(1)}, u32[]{:S(2)}, u32[]{:S(2)}) collective-permute-start(f32[2,256,512]{2,1,0:T(8,128)S(1)} %fusion.104), channel_id=1, source_target_pairs={{0,4},{4,8},{8,12},{12,16},{16,20},{20,24},{24,28},{28,32},{32,36}... | collective-permute-start | bytes 3145736 | tf_op jit(solution)/shard_map/while/body/eval_jaxpr/ppermute | solution.py:10
  402.1 18.3 %collective-permute-start.1 = (f32[2,256,512]{2,1,0:T(8,128)S(1)}, f32[2,256,512]{2,1,0:T(8,128)S(1)}, u32[]{:S(2)}, u32[]{:S(2)}) collective-permute-start(f32[2,256,512]{2,1,0:T(8,128)S(1)} %fusion.104), channel_id=1, source_target_pairs={{0,4},{4,8},{8,12},{12,16},{16,20},{20,24},{24,28},{28,32},{32,36}... | collective-permute-start | bytes 3145736 | tf_op jit(solution)/shard_map/while/body/eval_jaxpr/ppermute | solution.py:10
  423.0 18.3 %collective-permute-start.1 = (f32[2,256,512]{2,1,0:T(8,128)S(1)}, f32[2,256,512]{2,1,0:T(8,128)S(1)}, u32[]{:S(2)}, u32[]{:S(2)}) collective-permute-start(f32[2,256,512]{2,1,0:T(8,128)S(1)} %fusion.104), channel_id=1, source_target_pairs={{0,4},{4,8},{8,12},{12,16},{16,20},{20,24},{24,28},{28,32},{32,36}... | collective-permute-start | bytes 3145736 | tf_op jit(solution)/shard_map/while/body/eval_jaxpr/ppermute | solution.py:10
  443.9 18.3 %collective-permute-start.1 = (f32[2,256,512]{2,1,0:T(8,128)S(1)}, f32[2,256,512]{2,1,0:T(8,128)S(1)}, u32[]{:S(2)}, u32[]{:S(2)}) collective-permute-start(f32[2,256,512]{2,1,0:T(8,128)S(1)} %fusion.104), channel_id=1, source_target_pairs={{0,4},{4,8},{8,12},{12,16},{16,20},{20,24},{24,28},{28,32},{32,36}... | collective-permute-start | bytes 3145736 | tf_op jit(solution)/shard_map/while/body/eval_jaxpr/ppermute | solution.py:10
  464.8 18.3 %collective-permute-start.1 = (f32[2,256,512]{2,1,0:T(8,128)S(1)}, f32[2,256,512]{2,1,0:T(8,128)S(1)}, u32[]{:S(2)}, u32[]{:S(2)}) collective-permute-start(f32[2,256,512]{2,1,0:T(8,128)S(1)} %fusion.104), channel_id=1, source_target_pairs={{0,4},{4,8},{8,12},{12,16},{16,20},{20,24},{24,28},{28,32},{32,36}... | collective-permute-start | bytes 3145736 | tf_op jit(solution)/shard_map/while/body/eval_jaxpr/ppermute | solution.py:10
  485.7 18.3 %collective-permute-start.1 = (f32[2,256,512]{2,1,0:T(8,128)S(1)}, f32[2,256,512]{2,1,0:T(8,128)S(1)}, u32[]{:S(2)}, u32[]{:S(2)}) collective-permute-start(f32[2,256,512]{2,1,0:T(8,128)S(1)} %fusion.104), channel_id=1, source_target_pairs={{0,4},{4,8},{8,12},{12,16},{16,20},{20,24},{24,28},{28,32},{32,36}... | collective-permute-start | bytes 3145736 | tf_op jit(solution)/shard_map/while/body/eval_jaxpr/ppermute | solution.py:10
  506.6 18.3 %collective-permute-start.1 = (f32[2,256,512]{2,1,0:T(8,128)S(1)}, f32[2,256,512]{2,1,0:T(8,128)S(1)}, u32[]{:S(2)}, u32[]{:S(2)}) collective-permute-start(f32[2,256,512]{2,1,0:T(8,128)S(1)} %fusion.104), channel_id=1, source_target_pairs={{0,4},{4,8},{8,12},{12,16},{16,20},{20,24},{24,28},{28,32},{32,36}... | collective-permute-start | bytes 3145736 | tf_op jit(solution)/shard_map/while/body/eval_jaxpr/ppermute | solution.py:10
  527.5 18.3 %collective-permute-start.1 = (f32[2,256,512]{2,1,0:T(8,128)S(1)}, f32[2,256,512]{2,1,0:T(8,128)S(1)}, u32[]{:S(2)}, u32[]{:S(2)}) collective-permute-start(f32[2,256,512]{2,1,0:T(8,128)S(1)} %fusion.104), channel_id=1, source_target_pairs={{0,4},{4,8},{8,12},{12,16},{16,20},{20,24},{24,28},{28,32},{32,36}... | collective-permute-start | bytes 3145736 | tf_op jit(solution)/shard_map/while/body/eval_jaxpr/ppermute | solution.py:10
  548.4 18.3 %collective-permute-start.1 = (f32[2,256,512]{2,1,0:T(8,128)S(1)}, f32[2,256,512]{2,1,0:T(8,128)S(1)}, u32[]{:S(2)}, u32[]{:S(2)}) collective-permute-start(f32[2,256,512]{2,1,0:T(8,128)S(1)} %fusion.104), channel_id=1, source_target_pairs={{0,4},{4,8},{8,12},{12,16},{16,20},{20,24},{24,28},{28,32},{32,36}... | collective-permute-start | bytes 3145736 | tf_op jit(solution)/shard_map/while/body/eval_jaxpr/ppermute | solution.py:10
  569.4 18.3 %collective-permute-start.1 = (f32[2,256,512]{2,1,0:T(8,128)S(1)}, f32[2,256,512]{2,1,0:T(8,128)S(1)}, u32[]{:S(2)}, u32[]{:S(2)}) collective-permute-start(f32[2,256,512]{2,1,0:T(8,128)S(1)} %fusion.104), channel_id=1, source_target_pairs={{0,4},{4,8},{8,12},{12,16},{16,20},{20,24},{24,28},{28,32},{32,36}... | collective-permute-start | bytes 3145736 | tf_op jit(solution)/shard_map/while/body/eval_jaxpr/ppermute | solution.py:10
  590.3 18.3 %collective-permute-start.1 = (f32[2,256,512]{2,1,0:T(8,128)S(1)}, f32[2,256,512]{2,1,0:T(8,128)S(1)}, u32[]{:S(2)}, u32[]{:S(2)}) collective-permute-start(f32[2,256,512]{2,1,0:T(8,128)S(1)} %fusion.104), channel_id=1, source_target_pairs={{0,4},{4,8},{8,12},{12,16},{16,20},{20,24},{24,28},{28,32},{32,36}... | collective-permute-start | bytes 3145736 | tf_op jit(solution)/shard_map/while/body/eval_jaxpr/ppermute | solution.py:10
  611.2 18.3 %collective-permute-start.1 = (f32[2,256,512]{2,1,0:T(8,128)S(1)}, f32[2,256,512]{2,1,0:T(8,128)S(1)}, u32[]{:S(2)}, u32[]{:S(2)}) collective-permute-start(f32[2,256,512]{2,1,0:T(8,128)S(1)} %fusion.104), channel_id=1, source_target_pairs={{0,4},{4,8},{8,12},{12,16},{16,20},{20,24},{24,28},{28,32},{32,36}... | collective-permute-start | bytes 3145736 | tf_op jit(solution)/shard_map/while/body/eval_jaxpr/ppermute | solution.py:10
  632.1 18.3 %collective-permute-start.1 = (f32[2,256,512]{2,1,0:T(8,128)S(1)}, f32[2,256,512]{2,1,0:T(8,128)S(1)}, u32[]{:S(2)}, u32[]{:S(2)}) collective-permute-start(f32[2,256,512]{2,1,0:T(8,128)S(1)} %fusion.104), channel_id=1, source_target_pairs={{0,4},{4,8},{8,12},{12,16},{16,20},{20,24},{24,28},{28,32},{32,36}... | collective-permute-start | bytes 3145736 | tf_op jit(solution)/shard_map/while/body/eval_jaxpr/ppermute | solution.py:10
  653.0 18.3 %collective-permute-start.1 = (f32[2,256,512]{2,1,0:T(8,128)S(1)}, f32[2,256,512]{2,1,0:T(8,128)S(1)}, u32[]{:S(2)}, u32[]{:S(2)}) collective-permute-start(f32[2,256,512]{2,1,0:T(8,128)S(1)} %fusion.104), channel_id=1, source_target_pairs={{0,4},{4,8},{8,12},{12,16},{16,20},{20,24},{24,28},{28,32},{32,36}... | collective-permute-start | bytes 3145736 | tf_op jit(solution)/shard_map/while/body/eval_jaxpr/ppermute | solution.py:10
  673.9 18.3 %collective-permute-start.1 = (f32[2,256,512]{2,1,0:T(8,128)S(1)}, f32[2,256,512]{2,1,0:T(8,128)S(1)}, u32[]{:S(2)}, u32[]{:S(2)}) collective-permute-start(f32[2,256,512]{2,1,0:T(8,128)S(1)} %fusion.104), channel_id=1, source_target_pairs={{0,4},{4,8},{8,12},{12,16},{16,20},{20,24},{24,28},{28,32},{32,36}... | collective-permute-start | bytes 3145736 | tf_op jit(solution)/shard_map/while/body/eval_jaxpr/ppermute | solution.py:10
  (79 other events, 777.4 us)
Sparse Core Ops, SparseCore 0:
  714.4 101.9 reduce-scatter.1
where the time goes:
time: 827 us; the launch traced here: 823 us
  starting transfers between devices  477 us (58%)
  waiting for transfers between devices  169 us (20%)
  other arithmetic  87.7 us (11%)
  matrix products  59.7 us (7%)
  local copies, waits for them, and re-layouts  15.3 us (2%)
  between operations  13.5 us (2%)
    ppermute x93, starting transfers between devices, passed_along(): return lax.ppermute(block, axis, route)  477 us
    reduce_scatter x1, waiting for transfers between devices, on_device(): lax.psum_scatter(terms.astype(jnp.bfloat16), 'head', scatter_dimension=1,...  102 us
    ppermute x93, waiting for transfers between devices, passed_along(): return lax.ppermute(block, axis, route)  66.5 us
    add x31, other arithmetic, combine(): memory = weight_a[:, None, None] * mem_a + weight_b[:, None, None] * mem_b  45.2 us
    select_n x93, other arithmetic, relay(): jnp.where(leading, base, got)  33.4 us
  transfers between devices with their start and end apart: 94, of which 32 were waited for; matrix products, arithmetic and copies ran while one was open for 0% of the time, Pallas kernels for 0%

commit v1 on v0

v1 whole, which is shorter than its diff:
```python
import functools

import jax
import jax.numpy as jnp
from jax import lax
from jax.experimental import pallas as pl
from jax.experimental.pallas import tpu as pltpu
from jax.sharding import PartitionSpec as P

MESH = pl.DeviceIdType.MESH
F32, BF16 = jnp.float32, jnp.bfloat16
LOW = -1e30


def running(x, join, fill):
    lane = lax.broadcasted_iota(jnp.int32, x.shape, 1)
    step = 1
    while step < x.shape[1]:
        x = join(x, jnp.where(lane >= step, pltpu.roll(x, step, 1), fill))
        step *= 2
    return x


def log_sigmoid(x):
    e = jnp.exp(-jnp.abs(x))
    u = 1.0 + e
    tail = jnp.where(u == 1.0, e, jnp.log(u) * (e / jnp.where(u == 1.0, 1.0, u - 1.0)))
    return jnp.minimum(x, 0.0) - tail


def wide(row, width):
    return jnp.concatenate([row] * (width // row.shape[1]), axis=1)


def mix_kernel(
    q_hbm, k_hbm, v_hbm, gate_in, gate_f, hidden,
    qf, kf, vf, qc, kc, vb, num, den, gcol, grow, own_c, own_n, gone, gone_n, came, came_n,
    chip_c, chip_n, slots, slots_n, back, prefix, pre_n, fix, fix_n, out_c, out_n,
    load_sem, pair_sem, ss, rs, sns, rns, sb, rb,
):
    rows = q_hbm.shape[0]
    tile = 256
    ctx, y = lax.axis_index("ctx"), lax.axis_index("head")
    core = lax.rem(ctx, 2)
    chip = lax.div(ctx, 2)
    mate = ctx + 1 - 2 * core
    chips = slots.shape[0]
    part = slots.shape[1]

    loads = []
    for h in range(2):
        for j, (src, dst) in enumerate(((k_hbm, kf), (v_hbm, vf), (q_hbm, qf))):
            loads.append(pltpu.make_async_copy(src.at[:, h, :], dst.at[h], load_sem.at[h, j]))
    for c in (0, 1, 3, 4, 2, 5):
        loads[c].start()

    barrier = pltpu.get_barrier_semaphore()
    pl.semaphore_signal(barrier, inc=1, device_id=(mate, y), device_id_type=MESH)

    def greet(i, _):
        other = lax.rem(chip + i, chips) * 2 + core
        pl.semaphore_signal(barrier, inc=1, device_id=(other, y), device_id_type=MESH)
        return 0

    lax.fori_loop(1, chips, greet, 0)

    log_f = log_sigmoid(gate_f[...])
    cum = running(log_f, jnp.add, 0.0)
    g = gate_in[...] - cum
    peak = running(g, jnp.maximum, LOW)
    grow[0:2, :] = g
    gcol[...] = jnp.transpose(jnp.concatenate([g, peak, g, peak], axis=0), (1, 0))
    f_end = cum[:, rows - 1:rows]
    g_top = peak[:, rows - 1:rows]

    for h in range(2):
        loads[3 * h].wait()
        loads[3 * h + 1].wait()
        vb[h] = vf[h].astype(BF16)
        w = jnp.exp(gcol[:, h:h + 1] - g_top[h:h + 1, :])
        kw = kf[h] * w
        own_c[h] = lax.dot_general(
            kw.astype(BF16), vb[h], (((0,), (0,)), ((), ())), preferred_element_type=F32
        )
        n = jnp.sum(kw, axis=0, keepdims=True)
        own_n[h, 0:1, :] = n[:, :128]
        own_n[h, 1:2, :] = n[:, 128:]
        own_n[h, 2:3, :] = jnp.broadcast_to(f_end[h:h + 1, :], (1, 128))
        own_n[h, 3:4, :] = jnp.broadcast_to(g_top[h:h + 1, :] + f_end[h:h + 1, :], (1, 128))
        own_n[h, 4:8, :] = jnp.zeros((4, 128), F32)
    pl.semaphore_wait(barrier, chips)
    gone[...] = own_c[1 - core].astype(BF16)
    swap = [
        pltpu.make_async_remote_copy(
            src_ref=gone, dst_ref=came, send_sem=pair_sem.at[0], recv_sem=pair_sem.at[1],
            device_id=(mate, y), device_id_type=MESH),
        pltpu.make_async_remote_copy(
            src_ref=own_n.at[1 - core], dst_ref=came_n, send_sem=pair_sem.at[2], recv_sem=pair_sem.at[3],
            device_id=(mate, y), device_id_type=MESH),
    ]
    for c in swap:
        c.start()
    for c in swap:
        c.wait()

    mine_n, their_n = own_n[core], came_n[...]
    first = core == 0
    n0, n1 = jnp.where(first, mine_n, their_n), jnp.where(first, their_n, mine_n)
    f0, t0, f1, t1 = n0[2:3], n0[3:4], n1[2:3], n1[3:4]
    top = jnp.maximum(t0 + f1, t1)
    w0, w1 = jnp.exp(t0 + f1 - top), jnp.exp(t1 - top)
    w_mine, w_their = jnp.where(first, w0, w1), jnp.where(first, w1, w0)
    width = own_c.shape[2]
    chip_c[...] = (
        own_c[core] * wide(w_mine, width) + came[...].astype(F32) * wide(w_their, width)
    ).astype(BF16)
    chip_n[0:2, :] = n0[0:2] * w0 + n1[0:2] * w1
    chip_n[2:3, :] = f0 + f1
    chip_n[3:4, :] = top
    chip_n[4:8, :] = jnp.zeros((4, 128), F32)

    def to_owner(other):
        at = pl.ds(pl.multiple_of(other * part, part), part)
        who = (other * 2 + core, y)
        return (
            pltpu.make_async_remote_copy(
                src_ref=chip_n, dst_ref=slots_n.at[chip], send_sem=sns.at[other], recv_sem=rns.at[chip],
                device_id=who, device_id_type=MESH),
            pltpu.make_async_remote_copy(
                src_ref=chip_c.at[at], dst_ref=slots.at[chip], send_sem=ss.at[other], recv_sem=rs.at[chip],
                device_id=who, device_id_type=MESH),
        )

    def from_chip(other):
        who = (other * 2 + core, y)
        return (
            pltpu.make_async_remote_copy(
                src_ref=chip_n, dst_ref=slots_n.at[other], send_sem=sns.at[other], recv_sem=rns.at[other],
                device_id=who, device_id_type=MESH),
            pltpu.make_async_remote_copy(
                src_ref=chip_c.at[pl.ds(0, part)], dst_ref=slots.at[other], send_sem=ss.at[other],
                recv_sem=rs.at[other], device_id=who, device_id_type=MESH),
        )

    def send(i, _):
        for c in to_owner(lax.rem(chip + i, chips)):
            c.start()
        return 0

    lax.fori_loop(1, chips, send, 0)
    slots_n[chip] = chip_n[...]
    slots[chip] = chip_c[pl.ds(pl.multiple_of(chip * part, part), part), :]

    def attend(h):
        loads[3 * h + 2].wait()
        q = qf[h] * 0.0625
        q_hi = q.astype(BF16)
        q_lo = (q - q_hi.astype(F32)).astype(BF16)
        qf[h] = q
        qc[h, :, 0:256] = q_hi
        qc[h, :, 256:512] = q_hi
        qc[h, :, 512:768] = q_lo
        k = kf[h]
        k_hi = k.astype(BF16)
        k_lo = (k - k_hi.astype(F32)).astype(BF16)
        kc[:, 0:256] = k_hi
        kc[:, 256:512] = k_lo
        kc[:, 512:768] = k_hi
        for i in range(rows // tile):
            at = slice(i * tile, (i + 1) * tile)
            peak_col = gcol[at, 2 + h:3 + h]
            upto = (i + 1) * tile
            s = lax.dot_general(
                qc[h, at, :], kc[0:upto, :], (((1,), (1,)), ((), ())), preferred_element_type=F32
            )
            z = grow[h:h + 1, 0:upto] - peak_col
            r = lax.broadcasted_iota(jnp.int32, (tile, upto), 0) + i * tile
            c = lax.broadcasted_iota(jnp.int32, (tile, upto), 1)
            w = jnp.exp(jnp.where(c <= r, z, -jnp.inf)) * s
            den[h, at, :] = jnp.sum(w, axis=1, keepdims=True)
            num[h, at, :] = jnp.dot(w.astype(BF16), vb[h, 0:upto, :], preferred_element_type=F32)

    attend(0)

    def got_n(i, _):
        from_chip(lax.rem(chip + i, chips))[0].wait_recv()
        return 0

    lax.fori_loop(1, chips, got_n, 0)

    def got_c(i, _):
        from_chip(lax.rem(chip + i, chips))[1].wait_recv()
        return 0

    lax.fori_loop(1, chips, got_c, 0)

    def give_back(other):
        return pltpu.make_async_remote_copy(
            src_ref=back.at[other], dst_ref=prefix.at[pl.ds(pl.multiple_of(chip * part, part), part)],
            send_sem=sb.at[other], recv_sem=rb.at[chip], device_id=(other * 2 + core, y), device_id_type=MESH)

    def take_back(other):
        return pltpu.make_async_remote_copy(
            src_ref=back.at[other], dst_ref=prefix.at[pl.ds(pl.multiple_of(other * part, part), part)],
            send_sem=sb.at[other], recv_sem=rb.at[other], device_id=(other * 2 + core, y), device_id_type=MESH)

    def scan(p, carry):
        m, c, n = carry
        back[p] = c.astype(BF16)

        @pl.when(p == chip)
        def _():
            pre_n[0:2, :] = n
            pre_n[2:3, :] = m
            prefix[pl.ds(pl.multiple_of(chip * part, part), part), :] = c.astype(BF16)

        @pl.when(p != chip)
        def _():
            give_back(p).start()

        later = slots_n[p]
        f, t = later[2:3], later[3:4]
        top = jnp.maximum(m + f, t)
        a, b = jnp.exp(m + f - top), jnp.exp(t - top)
        c = c * wide(a, width) + slots[p].astype(F32) * wide(b, width)
        return top, c, n * a + later[0:2] * b

    lax.fori_loop(
        0, chips, scan,
        (jnp.full((1, 128), LOW, F32), jnp.zeros((part, width), F32), jnp.zeros((2, 128), F32)),
    )

    attend(1)

    def got_back(i, _):
        take_back(lax.rem(chip + i, chips)).wait_recv()
        return 0

    lax.fori_loop(1, chips, got_back, 0)

    pm, pn = pre_n[2:3, :], pre_n[0:2, :]
    top = jnp.maximum(pm + f0, t0)
    a, b = jnp.exp(pm + f0 - top), jnp.exp(t0 - top)
    zero = jnp.zeros_like(b)
    b_mine, b_their = jnp.where(first, b, zero), jnp.where(first, zero, b)
    p_c = prefix[...].astype(F32)
    second_c = (
        p_c * wide(a, width) + own_c[core] * wide(b_mine, width) + came[...].astype(F32) * wide(b_their, width)
    )
    second_n = pn * a + n0[0:2] * b
    fix[core] = jnp.where(first, p_c, second_c).astype(BF16)
    out_c[...] = jnp.where(first, second_c, p_c).astype(BF16)
    fix_n[core, 0:2, :] = jnp.where(first, pn, second_n)
    fix_n[core, 2:3, :] = jnp.where(first, pm, top)
    out_n[0:2, :] = jnp.where(first, second_n, pn)
    out_n[2:3, :] = jnp.where(first, top, pm)
    out_n[3:8, :] = jnp.zeros((5, 128), F32)
    fix_n[core, 3:8, :] = jnp.zeros((5, 128), F32)
    tell = [
        pltpu.make_async_remote_copy(
            src_ref=out_c, dst_ref=fix.at[core], send_sem=pair_sem.at[4], recv_sem=pair_sem.at[5],
            device_id=(mate, y), device_id_type=MESH),
        pltpu.make_async_remote_copy(
            src_ref=out_n, dst_ref=fix_n.at[core], send_sem=pair_sem.at[6], recv_sem=pair_sem.at[7],
            device_id=(mate, y), device_id_type=MESH),
    ]
    for c in tell:
        c.start()
    for c in tell:
        c.wait()

    for h in range(2):
        pm = fix_n[h, 2:3, 0:1]
        n_row = jnp.concatenate([fix_n[h, 0:1, :], fix_n[h, 1:2, :]], axis=1)
        for i in range(rows // tile):
            at = slice(i * tile, (i + 1) * tile)
            peak_col = gcol[at, 2 + h:3 + h]
            top = jnp.maximum(peak_col, pm)
            ow, iw = jnp.exp(peak_col - top), jnp.exp(pm - top)
            mem = jnp.dot(qc[h, at, 0:256], fix[h], preferred_element_type=F32)
            mem_n = jnp.sum(qf[h, at, :] * n_row, axis=1, keepdims=True)
            d = jnp.maximum(jnp.abs(ow * den[h, at, :] + iw * mem_n), 1.0)
            inv = 1.0 / d
            hidden[at, h * width:(h + 1) * width] = (
                (ow * inv) * num[h, at, :] + (iw * inv) * mem
            ).astype(BF16)

    def sent(i, _):
        other = lax.rem(chip + i, chips)
        for c in to_owner(other):
            c.wait_send()
        give_back(other).wait_send()
        return 0

    lax.fori_loop(1, chips, sent, 0)


def mix(queries, keys, values, gate_in, gate_f):
    rows, heads, dk = queries.shape
    dv = values.shape[2]
    chips = lax.axis_size("ctx") // 2
    part = dk // chips
    hbm = pl.BlockSpec(memory_space=pl.ANY)
    vmem = pl.BlockSpec(memory_space=pltpu.VMEM)
    V = pltpu.VMEM
    dma = pltpu.SemaphoreType.DMA
    return pl.pallas_call(
        mix_kernel,
        out_shape=jax.ShapeDtypeStruct((rows, heads * dv), BF16),
        in_specs=[hbm, hbm, hbm, vmem, vmem],
        out_specs=vmem,
        scratch_shapes=[
            V((heads, rows, dk), F32), V((heads, rows, dk), F32), V((heads, rows, dv), F32),
            V((heads, rows, 3 * dk), BF16), V((rows, 3 * dk), BF16), V((heads, rows, dv), BF16),
            V((heads, rows, dv), F32), V((heads, rows, 1), F32), V((rows, 8), F32), V((8, rows), F32),
            V((heads, dk, dv), F32), V((heads, 8, 128), F32), V((dk, dv), BF16), V((8, 128), F32),
            V((dk, dv), BF16), V((8, 128), F32),
            V((dk, dv), BF16), V((8, 128), F32), V((chips, part, dv), BF16), V((chips, 8, 128), F32),
            V((chips, part, dv), BF16), V((dk, dv), BF16), V((8, 128), F32),
            V((heads, dk, dv), BF16), V((heads, 8, 128), F32), V((dk, dv), BF16), V((8, 128), F32),
            dma((heads, 3)), dma((8,)), dma((chips,)), dma((chips,)), dma((chips,)), dma((chips,)),
            dma((chips,)), dma((chips,)),
        ],
        compiler_params=pltpu.CompilerParams(
            collective_id=0, has_side_effects=True, vmem_limit_bytes=60 << 20
        ),
        name="mix",
    )(queries, keys, values, gate_in, gate_f)


def on_device(queries, keys, values, entry_gate_logit, forget_gate, out_weight):
    hidden = mix(queries, keys, values, entry_gate_logit, forget_gate)
    terms = jnp.dot(hidden, out_weight, preferred_element_type=F32)
    return lax.psum_scatter(terms.astype(BF16), "head", scatter_dimension=1, tiled=True)


def solution(mesh):
    placed = (
        P("ctx", "head", None),
        P("ctx", "head", None),
        P("ctx", "head", None),
        P("head", "ctx"),
        P("head", "ctx"),
        P("head", None),
    )
    return jax.shard_map(
        on_device, mesh=mesh, in_specs=placed, out_specs=P("ctx", "head"), check_vma=False
    )
```

time: 827 us -> 137 us (0.17)
  starting transfers between devices: 477 us -> 0.01 us
  waiting for transfers between devices: 169 us -> 79.5 us
  other arithmetic: 87.7 us -> 0 us
  matrix products: 59.7 us -> 14.9 us
  Pallas kernels: 0 us -> 29.5 us
  local copies, waits for them, and re-layouts: 15.3 us -> 0 us
    ppermute x93 -> x0, starting transfers between devices: 477 us -> none  [passed_along(): return lax.ppermute(block, axis, route)]
    ppermute x93 -> x0, waiting for transfers between devices: 66.5 us -> none  [passed_along(): return lax.ppermute(block, axis, route)]
    add x64 -> x0, other arithmetic: 47.6 us -> none  [the longest x31 45.2 us: combine(): memory = weight_a[:, None, None] * mem_a + weight_b[:, None, None] * mem_b]
    dot_general x13 -> x1, matrix products: 59.7 us -> 14.9 us  [on_device(): terms = jnp.dot(hidden, out_weight, preferred_element_type=F32)]
    select_n x93 -> x0, other arithmetic: 33.4 us -> none  [relay(): jnp.where(leading, base, got)]
    pallas_call x0 -> x1, Pallas kernels: none -> 29.5 us  [mix(): pl.pallas_call(mix_kernel, out_shape=jax.ShapeDtypeStruct((rows, heads *...]
    reduce_scatter x1, waiting for transfers between devices: 102 us -> 79.5 us  [on_device(): lax.psum_scatter(terms.astype(BF16), 'head', scatter_dimension=1, tiled=T...]
  transfers between devices with their start and end apart: 94 -> 1, of which waited for: 32 -> 1; matrix products, arithmetic and copies ran while one was open for 0% -> 0% of each run, Pallas kernels for 0% -> 0%
where the time goes in v1:
time: 137 us
  waiting for transfers between devices  79.5 us (58%)
  Pallas kernels  29.5 us (22%)
  matrix products  14.9 us (11%)
  between operations  13.4 us (10%)
    reduce_scatter x1, waiting for transfers between devices, on_device(): lax.psum_scatter(terms.astype(BF16), 'head', scatter_dimension=1, tiled=T...  79.5 us
    pallas_call x1, Pallas kernels, mix(): pl.pallas_call(mix_kernel, out_shape=jax.ShapeDtypeStruct((rows, heads *...  29.5 us
    dot_general x1, matrix products, on_device(): terms = jnp.dot(hidden, out_weight, preferred_element_type=F32)  14.9 us
  transfers between devices with their start and end apart: 1, of which 1 were waited for; matrix products, arithmetic and copies ran while one was open for 0% of the time, Pallas kernels for 0%

profile of v1, /device:TPU:1, one launch (start us, length us, event | category | flops | bytes accessed | tf_op | source)
XLA Modules:
  0.0 137.3 jit_solution(5920110861896059880)
XLA Ops:
  6.5 0.0 reduce-scatter.2.cloned.1.call-start
  6.5 29.5 %mix.1 = bf16[1024,1024]{1,0:T(8,128)(2,1)} custom-call(f32[1024,2,256]{2,1,0:T(2,128)} %q_hbm.1, f32[1024,2,256]{2,1,0:T(2,128)} %k_hbm.1, f32[1024,2,512]{2,1,0:T(2,128)} %v_hbm.1, f32[2,1024]{1,0:T(2,128)} %gate_in.1, f32[2,1024]{1,0:T(2,128)} %gate_f.1), custom_call_target="tpu_custom_call" | custom-call | tf_op jit(solution)/shard_map/mix/pallas_call | solution.py:307
  36.0 14.9 %convolution_convert_fusion = bf16[1024,4096]{1,0:T(8,128)(2,1)} fusion(bf16[1024,1024]{1,0:T(8,128)(2,1)} %mix.1, bf16[1024,4096]{1,0:T(8,128)(2,1)} %param.11), kind=kOutput, calls=%fused_computation | convolution fusion | flops 8594128896 | bytes 18874368 | tf_op jit(solution)/shard_map/dot_general | solution.py:333
  50.9 0.0 reduce-scatter.2.cloned.1.call-update
  51.0 79.5 %reduce-scatter.2.cloned.1.call-done = bf16[1024,1024]{1,0:T(8,128)(2,1)} async-done(((bf16[1024,4096]{1,0:T(8,128)(2,1)}), bf16[1024,1024]{1,0:T(8,128)(2,1)}) %reduce-scatter.2.cloned.1.call-update) | async-done | bytes 2097168 | tf_op jit(solution)/shard_map/reduce_scatter | solution.py:334
Async XLA Ops:
  6.5 123.9 %reduce-scatter.2.cloned.1.call-start = ((), (), s32[]{:S(2)}) async-start(), calls=%async_computation.1 | async-start | bytes 10485760 | tf_op jit(solution)/shard_map/reduce_scatter | solution.py:334
Sparse Core Ops, SparseCore 0:
  51.1 79.3 reduce-scatter.1

commit v2 on v1

--- a/solution.py
+++ b/solution.py
@@ -32,11 +32,13 @@
     return jnp.concatenate([row] * (width // row.shape[1]), axis=1)
 
 
-def mix_kernel(
-    q_hbm, k_hbm, v_hbm, gate_in, gate_f, hidden,
+def layer_kernel(
+    q_hbm, k_hbm, v_hbm, w_hbm, gate_in, gate_f, out,
     qf, kf, vf, qc, kc, vb, num, den, gcol, grow, own_c, own_n, gone, gone_n, came, came_n,
     chip_c, chip_n, slots, slots_n, back, prefix, pre_n, fix, fix_n, out_c, out_n,
+    hidden, swapped, w_own, w_mate, y_out, y_in, z_out,
     load_sem, pair_sem, ss, rs, sns, rns, sb, rb,
+    fetch_s, fetch_r, ring_s, ring_r, share_s, share_r, xs, xr, ys, yr, zs, zr,
 ):
     rows = q_hbm.shape[0]
     tile = 256
@@ -46,6 +48,15 @@
     mate = ctx + 1 - 2 * core
     chips = slots.shape[0]
     part = slots.shape[1]
+    side = lax.rem(y, 2)
+    pair = lax.div(y, 2)
+    partner = y + 1 - 2 * side
+    across = 3 - y
+    kept = lax.rem(lax.div(y + 1, 2), 2)
+    cx, cz = lax.rem(chip, 4), lax.div(chip, 4)
+    half = rows // 2
+    cols = w_own.shape[2]
+    block = cols // 2
 
     loads = []
     for h in range(2):
@@ -53,9 +64,18 @@
             loads.append(pltpu.make_async_copy(src.at[:, h, :], dst.at[h], load_sem.at[h, j]))
     for c in (0, 1, 3, 4, 2, 5):
         loads[c].start()
+    w_loads = [
+        pltpu.make_async_copy(
+            w_hbm.at[:, pl.ds(pl.multiple_of((1 - pair if f == 0 else pair) * cols, cols), cols)],
+            w_own.at[f], load_sem.at[2, f])
+        for f in range(2)
+    ]
+    for c in w_loads:
+        c.start()
 
     barrier = pltpu.get_barrier_semaphore()
-    pl.semaphore_signal(barrier, inc=1, device_id=(mate, y), device_id_type=MESH)
+    for who in ((mate, y), (ctx, partner), (ctx, across)):
+        pl.semaphore_signal(barrier, inc=1, device_id=who, device_id_type=MESH)
 
     def greet(i, _):
         other = lax.rem(chip + i, chips) * 2 + core
@@ -63,6 +83,67 @@
         return 0
 
     lax.fori_loop(1, chips, greet, 0)
+
+    def strip(path, z_at, x_at, count=1):
+        at = z_at * 4 + x_at if path == 0 else x_at * 4 + z_at
+        return pl.ds(pl.multiple_of((core * 2 + path) * 256 + at * 16, 16), 16 * count)
+
+    def fetch(f, path):
+        at = strip(path, cz, cx)
+        col = (1 - pair if f == 0 else pair) * cols
+        return pltpu.make_async_remote_copy(
+            src_ref=w_hbm.at[at, pl.ds(pl.multiple_of(col, cols), cols)], dst_ref=w_mate.at[f, at],
+            send_sem=fetch_s.at[f, path], recv_sem=fetch_r.at[f, path], device_id=(ctx, partner), device_id_type=MESH)
+
+    def ring(f, path, stage, step, way, incoming):
+        along_x = (path == 0) == (stage == 0)
+        here = cx if along_x else cz
+        to = lax.rem(here + (1 if way == 0 else 3), 4)
+        back_by = step + (1 if incoming else 0)
+        owner = lax.rem(here + (4 - back_by if way == 0 else back_by), 4)
+        if stage == 0:
+            at = strip(path, cz, owner) if along_x else strip(path, owner, cx)
+        else:
+            at = strip(path, 0, owner, 4) if along_x else strip(path, owner, 0, 4)
+        width = cols if step == 0 else block
+        lo = 0 if step == 0 else way * block
+        ref = w_mate.at[f, at, pl.ds(lo, width)]
+        peer = (cz * 4 + to if along_x else to * 4 + cx) * 2 + core
+        i = stage * 4 + step * 2 + way
+        return pltpu.make_async_remote_copy(
+            src_ref=ref, dst_ref=ref, send_sem=ring_s.at[f, path, i], recv_sem=ring_r.at[f, path, i],
+            device_id=(peer, y), device_id_type=MESH)
+
+    def share(f, who):
+        ref = w_mate.at[f, pl.ds(pl.multiple_of(who * 512, 512), 512)]
+        return pltpu.make_async_remote_copy(
+            src_ref=ref, dst_ref=ref, send_sem=share_s.at[f], recv_sem=share_r.at[f],
+            device_id=(mate, y), device_id_type=MESH)
+
+    def gather(f, at):
+        if at == 0:
+            for path in range(2):
+                fetch(f, path).start()
+        for path in range(2):
+            if at == 1:
+                fetch(f, path).wait_recv()
+            if 2 <= at <= 5:
+                for way in range(2):
+                    ring(f, path, (at - 2) // 2, (at - 2) % 2, way, True).wait_recv()
+            if 1 <= at <= 4:
+                for way in range(2):
+                    ring(f, path, (at - 1) // 2, (at - 1) % 2, way, False).start()
+        if at == 5:
+            share(f, core).start()
+        if at == 6:
+            share(f, 1 - core).wait_recv()
+
+    def gather_sent(f):
+        for path in range(2):
+            fetch(f, path).wait_send()
+            for i in range(8):
+                ring(f, path, i // 4, (i // 2) % 2, i % 2, False).wait_send()
+        share(f, core).wait_send()
 
     log_f = log_sigmoid(gate_f[...])
     cum = running(log_f, jnp.add, 0.0)
@@ -71,6 +152,9 @@
     grow[0:2, :] = g
     gcol[...] = jnp.transpose(jnp.concatenate([g, peak, g, peak], axis=0), (1, 0))
     f_end = cum[:, rows - 1:rows]
+    pl.semaphore_wait(barrier, chips + 2)
+    gather(0, 0)
+    gather(1, 0)
     g_top = peak[:, rows - 1:rows]
 
     for h in range(2):
@@ -88,7 +172,7 @@
         own_n[h, 2:3, :] = jnp.broadcast_to(f_end[h:h + 1, :], (1, 128))
         own_n[h, 3:4, :] = jnp.broadcast_to(g_top[h:h + 1, :] + f_end[h:h + 1, :], (1, 128))
         own_n[h, 4:8, :] = jnp.zeros((4, 128), F32)
-    pl.semaphore_wait(barrier, chips)
+    gather(0, 1)
     gone[...] = own_c[1 - core].astype(BF16)
     swap = [
         pltpu.make_async_remote_copy(
@@ -148,10 +232,11 @@
         return 0
 
     lax.fori_loop(1, chips, send, 0)
+    gather(0, 2)
     slots_n[chip] = chip_n[...]
     slots[chip] = chip_c[pl.ds(pl.multiple_of(chip * part, part), part), :]
 
-    def attend(h):
+    def attend(h, between):
         loads[3 * h + 2].wait()
         q = qf[h] * 0.0625
         q_hi = q.astype(BF16)
@@ -179,8 +264,11 @@
             w = jnp.exp(jnp.where(c <= r, z, -jnp.inf)) * s
             den[h, at, :] = jnp.sum(w, axis=1, keepdims=True)
             num[h, at, :] = jnp.dot(w.astype(BF16), vb[h, 0:upto, :], preferred_element_type=F32)
-
-    attend(0)
+            if i == 2:
+                gather(0, between)
+
+    attend(0, 3)
+    gather(0, 4)
 
     def got_n(i, _):
         from_chip(lax.rem(chip + i, chips))[0].wait_recv()
@@ -230,7 +318,8 @@
         (jnp.full((1, 128), LOW, F32), jnp.zeros((part, width), F32), jnp.zeros((2, 128), F32)),
     )
 
-    attend(1)
+    attend(1, 5)
+    gather(1, 1)
 
     def got_back(i, _):
         take_back(lax.rem(chip + i, chips)).wait_recv()
@@ -269,11 +358,13 @@
     for c in tell:
         c.wait()
 
-    for h in range(2):
-        pm = fix_n[h, 2:3, 0:1]
-        n_row = jnp.concatenate([fix_n[h, 0:1, :], fix_n[h, 1:2, :]], axis=1)
-        for i in range(rows // tile):
-            at = slice(i * tile, (i + 1) * tile)
+    gather(1, 2)
+
+    def finish(start, count):
+        at = pl.ds(pl.multiple_of(start, 64), count)
+        for h in range(2):
+            pm = fix_n[h, 2:3, 0:1]
+            n_row = jnp.concatenate([fix_n[h, 0:1, :], fix_n[h, 1:2, :]], axis=1)
             peak_col = gcol[at, 2 + h:3 + h]
             top = jnp.maximum(peak_col, pm)
             ow, iw = jnp.exp(peak_col - top), jnp.exp(pm - top)
@@ -285,6 +376,118 @@
                 (ow * inv) * num[h, at, :] + (iw * inv) * mem
             ).astype(BF16)
 
+    chunks = ((0, 64, 1024), (64, 64, 1024), (128, 128, 512), (256, 256, 256))
+    y_first = (0, 2, 4, 8)
+
+    def x_copy(c):
+        start, count, _ = chunks[c]
+        src = hidden.at[pl.ds(pl.multiple_of((1 - kept) * half + start, 64), count)]
+        return pltpu.make_async_remote_copy(
+            src_ref=src, dst_ref=swapped.at[pl.ds(start, count)], send_sem=xs.at[c], recv_sem=xr.at[c],
+            device_id=(ctx, partner), device_id_type=MESH)
+
+    def y_copy(c, j, first):
+        start, count, w = chunks[c]
+        col = pl.multiple_of(lax.rem(first * block + j * w, cols), w)
+        at = (pl.ds(start, count), pl.ds(col, w))
+        return pltpu.make_async_remote_copy(
+            src_ref=y_out.at[at], dst_ref=y_in.at[at], send_sem=ys.at[y_first[c] + j],
+            recv_sem=yr.at[y_first[c] + j], device_id=(ctx, across), device_id_type=MESH)
+
+    def z_copy(c, j, incoming):
+        start, count, w = chunks[c]
+        rows_at = (1 - kept if incoming else kept) * half + start
+        return pltpu.make_async_remote_copy(
+            src_ref=z_out.at[pl.ds(start, count), pl.ds(pl.multiple_of(j * w, w), w)],
+            dst_ref=out.at[pl.ds(pl.multiple_of(rows_at, 64), count), pl.ds(pl.multiple_of(j * w, w), w)],
+            send_sem=zs.at[y_first[c] // 2 + j], recv_sem=zr.at[y_first[c] // 2 + j],
+            device_id=(ctx, partner), device_id_type=MESH)
+
+    def project(c, f, col):
+        start, count, w = chunks[c]
+        at = pl.ds(pl.multiple_of(kept * half + start, 64), count)
+        return jnp.dot(hidden[at, :], w_own[f, :, pl.ds(col, w)], preferred_element_type=F32) + jnp.dot(
+            swapped[pl.ds(start, count), :], w_mate[f, :, pl.ds(col, w)], preferred_element_type=F32)
+
+    def y_step(c):
+        start, count, w = chunks[c]
+        x_copy(c).wait_recv()
+
+        def one(j, _):
+            col = pl.multiple_of(lax.rem(side * block + j * w, cols), w)
+            y_out[pl.ds(start, count), pl.ds(col, w)] = project(c, 0, col).astype(BF16)
+            y_copy(c, j, side).start()
+            return 0
+
+        lax.fori_loop(0, cols // w, one, 0)
+
+    def f_step(c):
+        start, count, w = chunks[c]
+        per = block // w
+
+        def for_partner(j, _):
+            col = pl.multiple_of((1 - side) * block + j * w, w)
+            mine = project(c, 1, col)
+            y_copy(c, j, 1 - side).wait_recv()
+            z_out[pl.ds(start, count), pl.ds(pl.multiple_of(j * w, w), w)] = (
+                mine + y_in[pl.ds(start, count), pl.ds(col, w)].astype(F32)).astype(BF16)
+            z_copy(c, j, False).start()
+            return 0
+
+        lax.fori_loop(0, per, for_partner, 0)
+
+        def for_me(j, _):
+            col = pl.multiple_of(side * block + j * w, w)
+            mine = project(c, 1, col)
+            y_copy(c, j + per, 1 - side).wait_recv()
+            at = pl.ds(pl.multiple_of(kept * half + start, 64), count)
+            out[at, pl.ds(pl.multiple_of(j * w, w), w)] = (
+                mine + y_in[pl.ds(start, count), pl.ds(col, w)].astype(F32)).astype(BF16)
+            return 0
+
+        lax.fori_loop(0, per, for_me, 0)
+
+    for c in range(4):
+        finish((1 - kept) * half + chunks[c][0], chunks[c][1])
+        x_copy(c).start()
+        if c == 1:
+            finish(kept * half + chunks[0][0], chunks[0][1])
+    gather(1, 3)
+    for c in range(1, 4):
+        finish(kept * half + chunks[c][0], chunks[c][1])
+    w_loads[0].wait()
+    gather(0, 6)
+    y_step(0)
+    y_step(1)
+    gather(1, 4)
+    y_step(2)
+    gather(1, 5)
+    w_loads[1].wait()
+    gather(1, 6)
+    f_step(0)
+    f_step(1)
+    y_step(3)
+    f_step(2)
+    f_step(3)
+
+    gather_sent(0)
+    gather_sent(1)
+    for c in range(4):
+        x_copy(c).wait_send()
+        per = block // chunks[c][2]
+
+        def y_sent(j, _, c=c):
+            y_copy(c, j, side).wait_send()
+            return 0
+
+        def z_done(j, _, c=c):
+            z_copy(c, j, False).wait_send()
+            z_copy(c, j, True).wait_recv()
+            return 0
+
+        lax.fori_loop(0, 2 * per, y_sent, 0)
+        lax.fori_loop(0, per, z_done, 0)
+
     def sent(i, _):
         other = lax.rem(chip + i, chips)
         for c in to_owner(other):
@@ -295,7 +498,7 @@
     lax.fori_loop(1, chips, sent, 0)
 
 
-def mix(queries, keys, values, gate_in, gate_f):
+def layer(queries, keys, values, out_weight, gate_in, gate_f):
     rows, heads, dk = queries.shape
     dv = values.shape[2]
     chips = lax.axis_size("ctx") // 2
@@ -305,9 +508,9 @@
     V = pltpu.VMEM
     dma = pltpu.SemaphoreType.DMA
     return pl.pallas_call(
-        mix_kernel,
-        out_shape=jax.ShapeDtypeStruct((rows, heads * dv), BF16),
-        in_specs=[hbm, hbm, hbm, vmem, vmem],
+        layer_kernel,
+        out_shape=jax.ShapeDtypeStruct((rows, out_weight.shape[1] // 4), BF16),
+        in_specs=[hbm, hbm, hbm, hbm, vmem, vmem],
         out_specs=vmem,
         scratch_shapes=[
             V((heads, rows, dk), F32), V((heads, rows, dk), F32), V((heads, rows, dv), F32),
@@ -318,20 +521,24 @@
             V((dk, dv), BF16), V((8, 128), F32), V((chips, part, dv), BF16), V((chips, 8, 128), F32),
             V((chips, part, dv), BF16), V((dk, dv), BF16), V((8, 128), F32),
             V((heads, dk, dv), BF16), V((heads, 8, 128), F32), V((dk, dv), BF16), V((8, 128), F32),
-            dma((heads, 3)), dma((8,)), dma((chips,)), dma((chips,)), dma((chips,)), dma((chips,)),
+            V((rows, heads * dv), BF16), V((rows // 2, heads * dv), BF16),
+            V((2, heads * dv, out_weight.shape[1] // 2), BF16), V((2, heads * dv, out_weight.shape[1] // 2), BF16),
+            V((rows // 2, out_weight.shape[1] // 2), BF16), V((rows // 2, out_weight.shape[1] // 2), BF16),
+            V((rows // 2, out_weight.shape[1] // 4), BF16),
+            dma((3, 3)), dma((8,)), dma((chips,)), dma((chips,)), dma((chips,)), dma((chips,)),
             dma((chips,)), dma((chips,)),
+            dma((2, 2)), dma((2, 2)), dma((2, 2, 8)), dma((2, 2, 8)), dma((2,)), dma((2,)),
+            dma((4,)), dma((4,)), dma((16,)), dma((16,)), dma((8,)), dma((8,)),
         ],
         compiler_params=pltpu.CompilerParams(
             collective_id=0, has_side_effects=True, vmem_limit_bytes=60 << 20
         ),
-        name="mix",
-    )(queries, keys, values, gate_in, gate_f)
+        name="layer",
+    )(queries, keys, values, out_weight, gate_in, gate_f)
 
 
 def on_device(queries, keys, values, entry_gate_logit, forget_gate, out_weight):
-    hidden = mix(queries, keys, values, entry_gate_logit, forget_gate)
-    terms = jnp.dot(hidden, out_weight, preferred_element_type=F32)
-    return lax.psum_scatter(terms.astype(BF16), "head", scatter_dimension=1, tiled=True)
+    return layer(queries, keys, values, out_weight, entry_gate_logit, forget_gate)
 
 
 def solution(mesh):

time: 137 us -> 103 us (0.75); the launches traced: 137 us -> 102 us
  waiting for transfers between devices: 79.5 us -> 0 us
  Pallas kernels: 29.5 us -> 98.4 us
  matrix products: 14.9 us -> 0 us
  between operations: 13.4 us -> 0.01 us
  local copies, waits for them, and re-layouts: 0 us -> 3.08 us
    reduce_scatter x1 -> x0, waiting for transfers between devices: 79.5 us -> none  [on_device(): lax.psum_scatter(terms.astype(BF16), 'head', scatter_dimension=1, tiled=T...]
    pallas_call x1, Pallas kernels: 29.5 us -> 98.4 us  [layer(): pl.pallas_call(layer_kernel, out_shape=jax.ShapeDtypeStruct((rows, out_we...]
    dot_general x1 -> x0, matrix products: 14.9 us -> none  [on_device(): terms = jnp.dot(hidden, out_weight, preferred_element_type=F32)]
    unnamed x0 -> x1, local copies, waits for them, and re-layouts: none -> 3.08 us
  transfers between devices with their start and end apart: 1 -> 0, of which waited for: 1 -> 0; matrix products, arithmetic and copies ran while one was open for 0% -> 0% of each run, Pallas kernels for 0% -> 0%
where the time goes in v2:
time: 103 us; the launch traced here: 102 us
  Pallas kernels  98.4 us (96%)
  local copies, waits for them, and re-layouts  3.08 us (3%)
    pallas_call x1, Pallas kernels, layer(): pl.pallas_call(layer_kernel, out_shape=jax.ShapeDtypeStruct((rows, out_we...  98.4 us
    unnamed x1, local copies, waits for them, and re-layouts  3.08 us

profile of v2, /device:TPU:1, one launch (start us, length us, event | category | flops | bytes accessed | tf_op | source)
XLA Modules:
  0.0 101.5 jit_solution(3149361180873887154)
XLA Ops:
  0.0 98.4 %layer.1 = bf16[1024,1024]{1,0:T(8,128)(2,1)} custom-call(f32[1024,2,256]{2,1,0:T(2,128)} %q_hbm.1, f32[1024,2,256]{2,1,0:T(2,128)} %k_hbm.1, f32[1024,2,512]{2,1,0:T(2,128)} %v_hbm.1, bf16[1024,4096]{1,0:T(8,128)(2,1)} %w_hbm.1, f32[2,1024]{1,0:T(2,128)} %gate_in.1, f32[2,1024]{1,0:T(2,128)} %gate_f.1), custom_call_target="tpu_custom_call" | custom-call | tf_op jit(solution)/shard_map/layer/pallas_call | solution.py:510
  98.5 3.1 %copy.8 = bf16[1024,1024]{1,0:T(8,128)(2,1)} copy(bf16[1024,1024]{1,0:T(8,128)(2,1)} %layer.1) | data formatting | bytes 4194304

commit v3 on v1

--- a/solution.py
+++ b/solution.py
@@ -14,11 +14,22 @@
 
 def running(x, join, fill):
     lane = lax.broadcasted_iota(jnp.int32, x.shape, 1)
-    step = 1
-    while step < x.shape[1]:
+    row = lax.broadcasted_iota(jnp.int32, x.shape, 0)
+    for step in (1, 2, 4, 8, 16, 32, 64):
         x = join(x, jnp.where(lane >= step, pltpu.roll(x, step, 1), fill))
-        step *= 2
-    return x
+    ends = jnp.broadcast_to(x[:, 127:128], x.shape)
+    ends = jnp.where(row >= 2, pltpu.roll(ends, 2, 0), fill)
+    for step in (2, 4, 8):
+        ends = join(ends, jnp.where(row >= step, pltpu.roll(ends, step, 0), fill))
+    return join(x, ends)
+
+
+def stacked(x):
+    return jnp.concatenate([x[:, j:j + 128] for j in range(0, x.shape[1], 128)], axis=0)
+
+
+def unstacked(x):
+    return jnp.concatenate([x[j:j + 2, :] for j in range(0, x.shape[0], 2)], axis=1)
 
 
 def log_sigmoid(x):
@@ -32,11 +43,13 @@
     return jnp.concatenate([row] * (width // row.shape[1]), axis=1)
 
 
-def mix_kernel(
-    q_hbm, k_hbm, v_hbm, gate_in, gate_f, hidden,
+def layer_kernel(
+    q_hbm, k_hbm, v_hbm, w_hbm, gate_in, gate_f, out,
     qf, kf, vf, qc, kc, vb, num, den, gcol, grow, own_c, own_n, gone, gone_n, came, came_n,
     chip_c, chip_n, slots, slots_n, back, prefix, pre_n, fix, fix_n, out_c, out_n,
-    load_sem, pair_sem, ss, rs, sns, rns, sb, rb,
+    hidden, swapped, w_own, w_mate, y_out, y_in, z_out,
+    load_sem, w_sem, pair_sem, ss, rs, sns, rns, sb, rb,
+    fetch_s, fetch_r, ring_s, ring_r, share_s, share_r, xs, xr, ys, yr, zs, zr,
 ):
     rows = q_hbm.shape[0]
     tile = 256
@@ -46,6 +59,30 @@
     mate = ctx + 1 - 2 * core
     chips = slots.shape[0]
     part = slots.shape[1]
+    side = lax.rem(y, 2)
+    pair = lax.div(y, 2)
+    partner = y + 1 - 2 * side
+    across = 3 - y
+    kept = lax.rem(lax.div(y + 1, 2), 2)
+    cx, cz = lax.rem(chip, 4), lax.div(chip, 4)
+    half = rows // 2
+    block = w_own.shape[2]
+
+    def column(b, part_of, of_y):
+        other = of_y + 1 - 2 * part_of
+        start = (lax.div(of_y, 2) * -2 + 2 + part_of, lax.div(of_y, 2) * -2 + 3 - part_of, other, of_y)[b]
+        return start * block
+
+    barrier = pltpu.get_barrier_semaphore()
+    for who in ((mate, y), (ctx, partner), (ctx, across)):
+        pl.semaphore_signal(barrier, inc=1, device_id=who, device_id_type=MESH)
+
+    def greet(i, _):
+        other = lax.rem(chip + i, chips) * 2 + core
+        pl.semaphore_signal(barrier, inc=1, device_id=(other, y), device_id_type=MESH)
+        return 0
+
+    lax.fori_loop(1, chips, greet, 0)
 
     loads = []
     for h in range(2):
@@ -53,43 +90,93 @@
             loads.append(pltpu.make_async_copy(src.at[:, h, :], dst.at[h], load_sem.at[h, j]))
     for c in (0, 1, 3, 4, 2, 5):
         loads[c].start()
-
-    barrier = pltpu.get_barrier_semaphore()
-    pl.semaphore_signal(barrier, inc=1, device_id=(mate, y), device_id_type=MESH)
-
-    def greet(i, _):
-        other = lax.rem(chip + i, chips) * 2 + core
-        pl.semaphore_signal(barrier, inc=1, device_id=(other, y), device_id_type=MESH)
-        return 0
-
-    lax.fori_loop(1, chips, greet, 0)
-
-    log_f = log_sigmoid(gate_f[...])
-    cum = running(log_f, jnp.add, 0.0)
-    g = gate_in[...] - cum
+    w_loads = [
+        pltpu.make_async_copy(
+            w_hbm.at[:, pl.ds(pl.multiple_of(column(b, side, y), block), block)], w_own.at[b], w_sem.at[b])
+        for b in range(4)
+    ]
+
+    parts = ((0, 0, block // 2), (0, block // 2, block // 2), (1, 0, block), (2, 0, block), (3, 0, block))
+
+    def strip(f, path, z_at, x_at, count):
+        at = z_at * 4 + x_at if path == 0 else x_at * 4 + z_at
+        b, lo, width = parts[f]
+        return w_mate.at[
+            b, pl.ds(pl.multiple_of((core * 2 + path) * 256 + at * 16, 16), 16 * count), pl.ds(lo, width)]
+
+    def fetch(f, path):
+        at = cz * 4 + cx if path == 0 else cx * 4 + cz
+        b, lo, width = parts[f]
+        col = column(b, 1 - side, partner) + lo
+        return pltpu.make_async_remote_copy(
+            src_ref=w_hbm.at[
+                pl.ds(pl.multiple_of((core * 2 + path) * 256 + at * 16, 16), 16),
+                pl.ds(pl.multiple_of(col, 128), width)],
+            dst_ref=strip(f, path, cz, cx, 1),
+            send_sem=fetch_s.at[f, path], recv_sem=fetch_r.at[f, path], device_id=(ctx, partner), device_id_type=MESH)
+
+    def spread(f, path, stage, way, incoming):
+        along_x = (path == 0) == (stage == 0)
+        here = cx if along_x else cz
+        to = lax.rem(here + way, 4)
+        owner = lax.rem(here + 4 - way, 4) if incoming else here
+        if stage == 0:
+            ref = strip(f, path, cz, owner, 1) if along_x else strip(f, path, owner, cx, 1)
+        else:
+            ref = strip(f, path, 0, owner, 4) if along_x else strip(f, path, owner, 0, 4)
+        peer = (cz * 4 + to if along_x else to * 4 + cx) * 2 + core
+        i = stage * 3 + way - 1
+        return pltpu.make_async_remote_copy(
+            src_ref=ref, dst_ref=ref, send_sem=ring_s.at[f, path, i], recv_sem=ring_r.at[f, path, i],
+            device_id=(peer, y), device_id_type=MESH)
+
+    def share(f, who):
+        b, lo, width = parts[f]
+        ref = w_mate.at[b, pl.ds(pl.multiple_of(who * 512, 512), 512), pl.ds(lo, width)]
+        return pltpu.make_async_remote_copy(
+            src_ref=ref, dst_ref=ref, send_sem=share_s.at[f], recv_sem=share_r.at[f],
+            device_id=(mate, y), device_id_type=MESH)
+
+    def gather(f, *steps):
+        for step in steps:
+            for path in range(2):
+                if step == 0:
+                    fetch(f, path).start()
+                if step == 1:
+                    fetch(f, path).wait_recv()
+                for way in (1, 3, 2):
+                    if step == 2 or step == 3:
+                        spread(f, path, step - 2, way, True).wait_recv()
+                for way in (1, 3, 2):
+                    if step == 1 or step == 2:
+                        spread(f, path, step - 1, way, False).start()
+            if step == 3:
+                share(f, core).start()
+            if step == 4:
+                share(f, 1 - core).wait_recv()
+
+    def gather_sent(f):
+        for path in range(2):
+            fetch(f, path).wait_send()
+            for i in range(6):
+                spread(f, path, i // 3, i % 3 + 1, False).wait_send()
+        share(f, core).wait_send()
+
+    pl.semaphore_wait(barrier, chips + 2)
+    gather(0, 0)
+    gather(1, 0)
+    for c in w_loads:
+        c.start()
+    cum = running(log_sigmoid(stacked(gate_f[...])), jnp.add, 0.0)
+    g = stacked(gate_in[...]) - cum
     peak = running(g, jnp.maximum, LOW)
+    f_end = cum[14:16, 127:128]
+    g_top = peak[14:16, 127:128]
+    g, peak = unstacked(g), unstacked(peak)
     grow[0:2, :] = g
     gcol[...] = jnp.transpose(jnp.concatenate([g, peak, g, peak], axis=0), (1, 0))
-    f_end = cum[:, rows - 1:rows]
-    g_top = peak[:, rows - 1:rows]
-
-    for h in range(2):
-        loads[3 * h].wait()
-        loads[3 * h + 1].wait()
-        vb[h] = vf[h].astype(BF16)
-        w = jnp.exp(gcol[:, h:h + 1] - g_top[h:h + 1, :])
-        kw = kf[h] * w
-        own_c[h] = lax.dot_general(
-            kw.astype(BF16), vb[h], (((0,), (0,)), ((), ())), preferred_element_type=F32
-        )
-        n = jnp.sum(kw, axis=0, keepdims=True)
-        own_n[h, 0:1, :] = n[:, :128]
-        own_n[h, 1:2, :] = n[:, 128:]
-        own_n[h, 2:3, :] = jnp.broadcast_to(f_end[h:h + 1, :], (1, 128))
-        own_n[h, 3:4, :] = jnp.broadcast_to(g_top[h:h + 1, :] + f_end[h:h + 1, :], (1, 128))
-        own_n[h, 4:8, :] = jnp.zeros((4, 128), F32)
-    pl.semaphore_wait(barrier, chips)
-    gone[...] = own_c[1 - core].astype(BF16)
+    for c in (0, 1, 3, 4):
+        loads[c].wait()
     swap = [
         pltpu.make_async_remote_copy(
             src_ref=gone, dst_ref=came, send_sem=pair_sem.at[0], recv_sem=pair_sem.at[1],
@@ -98,8 +185,28 @@
             src_ref=own_n.at[1 - core], dst_ref=came_n, send_sem=pair_sem.at[2], recv_sem=pair_sem.at[3],
             device_id=(mate, y), device_id_type=MESH),
     ]
-    for c in swap:
-        c.start()
+    for turn, h in enumerate((1 - core, core)):
+        lead = h == 0
+        vb[h] = vf[h].astype(BF16)
+        top = jnp.where(lead, g_top[0:1, :], g_top[1:2, :])
+        end = jnp.where(lead, f_end[0:1, :], f_end[1:2, :])
+        w = jnp.exp(jnp.where(lead, gcol[:, 0:1], gcol[:, 1:2]) - top)
+        kw = kf[h] * w
+        state = lax.dot_general(
+            kw.astype(BF16), vb[h], (((0,), (0,)), ((), ())), preferred_element_type=F32
+        )
+        n = jnp.sum(kw, axis=0, keepdims=True)
+        own_n[h, 0:1, :] = n[:, :128]
+        own_n[h, 1:2, :] = n[:, 128:]
+        own_n[h, 2:3, :] = jnp.broadcast_to(end, (1, 128))
+        own_n[h, 3:4, :] = jnp.broadcast_to(top + end, (1, 128))
+        if turn == 0:
+            gone[...] = state.astype(BF16)
+            for c in swap:
+                c.start()
+        else:
+            own_c[...] = state
+    gather(0, 1)
     for c in swap:
         c.wait()
 
@@ -110,14 +217,13 @@
     top = jnp.maximum(t0 + f1, t1)
     w0, w1 = jnp.exp(t0 + f1 - top), jnp.exp(t1 - top)
     w_mine, w_their = jnp.where(first, w0, w1), jnp.where(first, w1, w0)
-    width = own_c.shape[2]
+    width = own_c.shape[1]
     chip_c[...] = (
-        own_c[core] * wide(w_mine, width) + came[...].astype(F32) * wide(w_their, width)
+        own_c[...] * wide(w_mine, width) + came[...].astype(F32) * wide(w_their, width)
     ).astype(BF16)
     chip_n[0:2, :] = n0[0:2] * w0 + n1[0:2] * w1
     chip_n[2:3, :] = f0 + f1
     chip_n[3:4, :] = top
-    chip_n[4:8, :] = jnp.zeros((4, 128), F32)
 
     def to_owner(other):
         at = pl.ds(pl.multiple_of(other * part, part), part)
@@ -180,7 +286,11 @@
             den[h, at, :] = jnp.sum(w, axis=1, keepdims=True)
             num[h, at, :] = jnp.dot(w.astype(BF16), vb[h, 0:upto, :], preferred_element_type=F32)
 
+    for f in range(2, 5):
+        gather(f, 0)
     attend(0)
+    gather(1, 1)
+    gather(0, 2)
 
     def got_n(i, _):
         from_chip(lax.rem(chip + i, chips))[0].wait_recv()
@@ -231,6 +341,7 @@
     )
 
     attend(1)
+    gather(2, 1)
 
     def got_back(i, _):
         take_back(lax.rem(chip + i, chips)).wait_recv()
@@ -238,6 +349,8 @@
 
     lax.fori_loop(1, chips, got_back, 0)
 
+    gather(0, 3)
+    gather(1, 2)
     pm, pn = pre_n[2:3, :], pre_n[0:2, :]
     top = jnp.maximum(pm + f0, t0)
     a, b = jnp.exp(pm + f0 - top), jnp.exp(t0 - top)
@@ -245,7 +358,7 @@
     b_mine, b_their = jnp.where(first, b, zero), jnp.where(first, zero, b)
     p_c = prefix[...].astype(F32)
     second_c = (
-        p_c * wide(a, width) + own_c[core] * wide(b_mine, width) + came[...].astype(F32) * wide(b_their, width)
+        p_c * wide(a, width) + own_c[...] * wide(b_mine, width) + came[...].astype(F32) * wide(b_their, width)
     )
     second_n = pn * a + n0[0:2] * b
     fix[core] = jnp.where(first, p_c, second_c).astype(BF16)
@@ -254,8 +367,7 @@
     fix_n[core, 2:3, :] = jnp.where(first, pm, top)
     out_n[0:2, :] = jnp.where(first, second_n, pn)
     out_n[2:3, :] = jnp.where(first, top, pm)
-    out_n[3:8, :] = jnp.zeros((5, 128), F32)
-    fix_n[core, 3:8, :] = jnp.zeros((5, 128), F32)
+    out_n[3:4, :] = jnp.zeros((1, 128), F32)
     tell = [
         pltpu.make_async_remote_copy(
             src_ref=out_c, dst_ref=fix.at[core], send_sem=pair_sem.at[4], recv_sem=pair_sem.at[5],
@@ -269,11 +381,11 @@
     for c in tell:
         c.wait()
 
-    for h in range(2):
-        pm = fix_n[h, 2:3, 0:1]
-        n_row = jnp.concatenate([fix_n[h, 0:1, :], fix_n[h, 1:2, :]], axis=1)
-        for i in range(rows // tile):
-            at = slice(i * tile, (i + 1) * tile)
+    def finish(start, count):
+        at = pl.ds(pl.multiple_of(start, 64), count)
+        for h in range(2):
+            pm = fix_n[h, 2:3, 0:1]
+            n_row = jnp.concatenate([fix_n[h, 0:1, :], fix_n[h, 1:2, :]], axis=1)
             peak_col = gcol[at, 2 + h:3 + h]
             top = jnp.maximum(peak_col, pm)
             ow, iw = jnp.exp(peak_col - top), jnp.exp(pm - top)
@@ -285,6 +397,158 @@
                 (ow * inv) * num[h, at, :] + (iw * inv) * mem
             ).astype(BF16)
 
+    small, count = 64, 4
+    big = half - small * count
+
+    def rows_at(mine, c):
+        base = (kept if mine else 1 - kept) * half
+        return base + c * small, (small if c is not count else big)
+
+    def x_copy(c):
+        start, size = rows_at(False, c)
+        return pltpu.make_async_remote_copy(
+            src_ref=hidden.at[pl.ds(pl.multiple_of(start, small), size)],
+            dst_ref=swapped.at[pl.ds(pl.multiple_of(c * small, small), size)], send_sem=xs.at[c], recv_sem=xr.at[c],
+            device_id=(ctx, partner), device_id_type=MESH)
+
+    def small_piece(c, p):
+        lo, w = ((0, block // 2), (block // 2, block // 2), (0, block))[p]
+        return c, p // 2, lo, w, c * 3 + p
+
+    def big_piece(b, j):
+        w = block // 4
+        return count, b, pl.multiple_of(j * w, w), w, 3 * count + b * 4 + j
+
+    def y_copy(piece):
+        c, b, lo, w, i = piece
+        at = (b, pl.ds(pl.multiple_of(c * small, small), rows_at(True, c)[1]), pl.ds(lo, w))
+        return pltpu.make_async_remote_copy(
+            src_ref=y_out.at[at], dst_ref=y_in.at[at], send_sem=ys.at[i], recv_sem=yr.at[i],
+            device_id=(ctx, across), device_id_type=MESH)
+
+    def z_copy(piece, incoming):
+        c, b, lo, w, i = piece
+        start, size = rows_at(not incoming, c)
+        return pltpu.make_async_remote_copy(
+            src_ref=z_out.at[pl.ds(pl.multiple_of(c * small, small), size), pl.ds(lo, w)],
+            dst_ref=out.at[pl.ds(pl.multiple_of(start, small), size), pl.ds(lo, w)],
+            send_sem=zs.at[i], recv_sem=zr.at[i], device_id=(ctx, partner), device_id_type=MESH)
+
+    def project(f, piece):
+        c, b, lo, w, i = piece
+        start, size = rows_at(True, c)
+        return jnp.dot(
+            hidden[pl.ds(pl.multiple_of(start, small), size), :], w_own[f, :, pl.ds(lo, w)],
+            preferred_element_type=F32,
+        ) + jnp.dot(
+            swapped[pl.ds(pl.multiple_of(c * small, small), size), :], w_mate[f, :, pl.ds(lo, w)],
+            preferred_element_type=F32,
+        )
+
+    def y_step(piece):
+        c, b, lo, w, i = piece
+        y_out[b, pl.ds(pl.multiple_of(c * small, small), rows_at(True, c)[1]), pl.ds(lo, w)] = project(b, piece).astype(BF16)
+        y_copy(piece).start()
+
+    def f_step(piece):
+        c, b, lo, w, i = piece
+        start, size = rows_at(True, c)
+        mine = project(2 + b, piece)
+        y_copy(piece).wait_recv()
+        at = pl.ds(pl.multiple_of(c * small, small), size)
+        total = (mine + y_in[b, at, pl.ds(lo, w)].astype(F32)).astype(BF16)
+        if b == 0:
+            z_out[at, pl.ds(lo, w)] = total
+            z_copy(piece, False).start()
+        else:
+            out[pl.ds(pl.multiple_of(start, small), size), pl.ds(lo, w)] = total
+
+    def each(n, body):
+        def one(i, _):
+            body(i)
+            return 0
+
+        lax.fori_loop(0, n, one, 0)
+
+    def finish_chunk(mine, c):
+        finish(*rows_at(mine, c))
+        if not mine:
+            x_copy(c).start()
+
+    finish_chunk(False, 0)
+    finish_chunk(True, 0)
+    each(count - 1, lambda i: finish_chunk(False, i + 1))
+    gather(2, 2)
+    gather(3, 1)
+    finish_chunk(False, count)
+    each(count - 1, lambda i: finish_chunk(True, i + 1))
+    finish_chunk(True, count)
+    for c in w_loads:
+        c.wait()
+    gather(1, 3)
+    gather(0, 4)
+
+    def first_columns(c):
+        x_copy(c).wait_recv()
+        y_step(small_piece(c, 0))
+
+        @pl.when(c == 0)
+        def _():
+            gather(1, 4)
+
+        y_step(small_piece(c, 1))
+
+        @pl.when(c == 1)
+        def _():
+            gather(3, 2)
+            gather(4, 1)
+
+        @pl.when(c == 2)
+        def _():
+            gather(2, 3)
+
+    each(count, first_columns)
+    gather(2, 4)
+    each(count, lambda c: y_step(small_piece(c, 2)))
+    gather(3, 3)
+    gather(4, 2)
+    gather(3, 4)
+
+    def for_partner(c):
+        f_step(small_piece(c, 0))
+        f_step(small_piece(c, 1))
+
+    each(count, for_partner)
+    x_copy(count).wait_recv()
+    each(4, lambda j: y_step(big_piece(0, j)))
+    each(4, lambda j: y_step(big_piece(1, j)))
+    gather(4, 3)
+    gather(4, 4)
+    each(count, lambda c: f_step(small_piece(c, 2)))
+    each(4, lambda j: f_step(big_piece(0, j)))
+    each(4, lambda j: f_step(big_piece(1, j)))
+
+    for f in range(5):
+        gather_sent(f)
+
+    def small_done(c):
+        x_copy(c).wait_send()
+        for p in range(3):
+            y_copy(small_piece(c, p)).wait_send()
+        for p in range(2):
+            z_copy(small_piece(c, p), False).wait_send()
+            z_copy(small_piece(c, p), True).wait_recv()
+
+    def big_done(j):
+        y_copy(big_piece(0, j)).wait_send()
+        y_copy(big_piece(1, j)).wait_send()
+        z_copy(big_piece(0, j), False).wait_send()
+        z_copy(big_piece(0, j), True).wait_recv()
+
+    each(count, small_done)
+    x_copy(count).wait_send()
+    each(4, big_done)
+
     def sent(i, _):
         other = lax.rem(chip + i, chips)
         for c in to_owner(other):
@@ -295,7 +559,7 @@
     lax.fori_loop(1, chips, sent, 0)
 
 
-def mix(queries, keys, values, gate_in, gate_f):
+def layer(queries, keys, values, out_weight, gate_in, gate_f):
     rows, heads, dk = queries.shape
     dv = values.shape[2]
     chips = lax.axis_size("ctx") // 2
@@ -305,33 +569,37 @@
     V = pltpu.VMEM
     dma = pltpu.SemaphoreType.DMA
     return pl.pallas_call(
-        mix_kernel,
-        out_shape=jax.ShapeDtypeStruct((rows, heads * dv), BF16),
-        in_specs=[hbm, hbm, hbm, vmem, vmem],
+        layer_kernel,
+        out_shape=jax.ShapeDtypeStruct((rows, out_weight.shape[1] // 4), BF16),
+        in_specs=[hbm, hbm, hbm, hbm, vmem, vmem],
         out_specs=vmem,
         scratch_shapes=[
             V((heads, rows, dk), F32), V((heads, rows, dk), F32), V((heads, rows, dv), F32),
             V((heads, rows, 3 * dk), BF16), V((rows, 3 * dk), BF16), V((heads, rows, dv), BF16),
             V((heads, rows, dv), F32), V((heads, rows, 1), F32), V((rows, 8), F32), V((8, rows), F32),
-            V((heads, dk, dv), F32), V((heads, 8, 128), F32), V((dk, dv), BF16), V((8, 128), F32),
-            V((dk, dv), BF16), V((8, 128), F32),
-            V((dk, dv), BF16), V((8, 128), F32), V((chips, part, dv), BF16), V((chips, 8, 128), F32),
-            V((chips, part, dv), BF16), V((dk, dv), BF16), V((8, 128), F32),
-            V((heads, dk, dv), BF16), V((heads, 8, 128), F32), V((dk, dv), BF16), V((8, 128), F32),
-            dma((heads, 3)), dma((8,)), dma((chips,)), dma((chips,)), dma((chips,)), dma((chips,)),
+            V((dk, dv), F32), V((heads, 4, 128), F32), V((dk, dv), BF16), V((4, 128), F32),
+            V((dk, dv), BF16), V((4, 128), F32),
+            V((dk, dv), BF16), V((4, 128), F32), V((chips, part, dv), BF16), V((chips, 4, 128), F32),
+            V((chips, part, dv), BF16), V((dk, dv), BF16), V((4, 128), F32),
+            V((heads, dk, dv), BF16), V((heads, 4, 128), F32), V((dk, dv), BF16), V((4, 128), F32),
+            V((rows, heads * dv), BF16), V((rows // 2, heads * dv), BF16),
+            V((4, heads * dv, out_weight.shape[1] // 4), BF16), V((4, heads * dv, out_weight.shape[1] // 4), BF16),
+            V((2, rows // 2, out_weight.shape[1] // 4), BF16), V((2, rows // 2, out_weight.shape[1] // 4), BF16),
+            V((rows // 2, out_weight.shape[1] // 4), BF16),
+            dma((2, 3)), dma((4,)), dma((8,)), dma((chips,)), dma((chips,)), dma((chips,)), dma((chips,)),
             dma((chips,)), dma((chips,)),
+            dma((5, 2)), dma((5, 2)), dma((5, 2, 6)), dma((5, 2, 6)), dma((5,)), dma((5,)),
+            dma((5,)), dma((5,)), dma((20,)), dma((20,)), dma((20,)), dma((20,)),
         ],
         compiler_params=pltpu.CompilerParams(
             collective_id=0, has_side_effects=True, vmem_limit_bytes=60 << 20
         ),
-        name="mix",
-    )(queries, keys, values, gate_in, gate_f)
+        name="layer",
+    )(queries, keys, values, out_weight, gate_in, gate_f)
 
 
 def on_device(queries, keys, values, entry_gate_logit, forget_gate, out_weight):
-    hidden = mix(queries, keys, values, entry_gate_logit, forget_gate)
-    terms = jnp.dot(hidden, out_weight, preferred_element_type=F32)
-    return lax.psum_scatter(terms.astype(BF16), "head", scatter_dimension=1, tiled=True)
+    return layer(queries, keys, values, out_weight, entry_gate_logit, forget_gate)
 
 
 def solution(mesh):

time: 137 us -> 91.4 us (0.67)
  waiting for transfers between devices: 79.5 us -> 0 us
  Pallas kernels: 29.5 us -> 88.1 us
  matrix products: 14.9 us -> 0 us
  between operations: 13.4 us -> 0.01 us
  local copies, waits for them, and re-layouts: 0 us -> 3.08 us
    reduce_scatter x1 -> x0, waiting for transfers between devices: 79.5 us -> none  [on_device(): lax.psum_scatter(terms.astype(BF16), 'head', scatter_dimension=1, tiled=T...]
    pallas_call x1, Pallas kernels: 29.5 us -> 88.1 us  [layer(): pl.pallas_call(layer_kernel, out_shape=jax.ShapeDtypeStruct((rows, out_we...]
    dot_general x1 -> x0, matrix products: 14.9 us -> none  [on_device(): terms = jnp.dot(hidden, out_weight, preferred_element_type=F32)]
    unnamed x0 -> x1, local copies, waits for them, and re-layouts: none -> 3.08 us
  transfers between devices with their start and end apart: 1 -> 0, of which waited for: 1 -> 0; matrix products, arithmetic and copies ran while one was open for 0% -> 0% of each run, Pallas kernels for 0% -> 0%
where the time goes in v3:
time: 91.4 us; the launch traced here: 91.2 us
  Pallas kernels  88.1 us (96%)
  local copies, waits for them, and re-layouts  3.08 us (3%)
    pallas_call x1, Pallas kernels, layer(): pl.pallas_call(layer_kernel, out_shape=jax.ShapeDtypeStruct((rows, out_we...  88.1 us
    unnamed x1, local copies, waits for them, and re-layouts  3.08 us

profile of v3, /device:TPU:1, one launch (start us, length us, event | category | flops | bytes accessed | tf_op | source)
XLA Modules:
  0.0 91.2 jit_solution(1969944196159478614)
XLA Ops:
  0.0 88.1 %layer.1 = bf16[1024,1024]{1,0:T(8,128)(2,1)} custom-call(f32[1024,2,256]{2,1,0:T(2,128)} %q_hbm.1, f32[1024,2,256]{2,1,0:T(2,128)} %k_hbm.1, f32[1024,2,512]{2,1,0:T(2,128)} %v_hbm.1, bf16[1024,4096]{1,0:T(8,128)(2,1)} %w_hbm.1, f32[2,1024]{1,0:T(2,128)} %gate_in.1, f32[2,1024]{1,0:T(2,128)} %gate_f.1), custom_call_target="tpu_custom_call" | custom-call | tf_op jit(solution)/shard_map/layer/pallas_call | solution.py:571
  88.1 3.1 %copy.8 = bf16[1024,1024]{1,0:T(8,128)(2,1)} copy(bf16[1024,1024]{1,0:T(8,128)(2,1)} %layer.1) | data formatting | bytes 4194304

commit v4 on v3

--- a/solution.py
+++ b/solution.py
@@ -44,11 +44,12 @@
 
 
 def layer_kernel(
-    q_hbm, k_hbm, v_hbm, w_hbm, gate_in, gate_f, out,
+    q_hbm, k_hbm, v_hbm, w_hbm, in_hbm, f_hbm, out,
+    gate_in, gate_f,
     qf, kf, vf, qc, kc, vb, num, den, gcol, grow, own_c, own_n, gone, gone_n, came, came_n,
     chip_c, chip_n, slots, slots_n, back, prefix, pre_n, fix, fix_n, out_c, out_n,
     hidden, swapped, w_own, w_mate, y_out, y_in, z_out,
-    load_sem, w_sem, pair_sem, ss, rs, sns, rns, sb, rb,
+    e_out, e_in, e_sum, e_got, e_sum2, edge_s, edge_r, edge_k, out_own, gate_sem, own_sem, load_sem, w_sem, pair_sem, ss, rs, sns, rns, sb, rb,
     fetch_s, fetch_r, ring_s, ring_r, share_s, share_r, xs, xr, ys, yr, zs, zr,
 ):
     rows = q_hbm.shape[0]
@@ -73,23 +74,29 @@
         start = (lax.div(of_y, 2) * -2 + 2 + part_of, lax.div(of_y, 2) * -2 + 3 - part_of, other, of_y)[b]
         return start * block
 
-    barrier = pltpu.get_barrier_semaphore()
-    for who in ((mate, y), (ctx, partner), (ctx, across)):
-        pl.semaphore_signal(barrier, inc=1, device_id=who, device_id_type=MESH)
-
-    def greet(i, _):
-        other = lax.rem(chip + i, chips) * 2 + core
-        pl.semaphore_signal(barrier, inc=1, device_id=(other, y), device_id_type=MESH)
-        return 0
-
-    lax.fori_loop(1, chips, greet, 0)
-
+    gates = [
+        pltpu.make_async_copy(f_hbm, gate_f, gate_sem.at[0]),
+        pltpu.make_async_copy(in_hbm, gate_in, gate_sem.at[1]),
+    ]
+    for c in gates:
+        c.start()
     loads = []
     for h in range(2):
         for j, (src, dst) in enumerate(((k_hbm, kf), (v_hbm, vf), (q_hbm, qf))):
             loads.append(pltpu.make_async_copy(src.at[:, h, :], dst.at[h], load_sem.at[h, j]))
     for c in (0, 1, 3, 4, 2, 5):
         loads[c].start()
+    barrier = pltpu.get_barrier_semaphore()
+    for who in ((mate, y), (ctx, partner), (ctx, across)):
+        pl.semaphore_signal(barrier, inc=1, device_id=who, device_id_type=MESH)
+
+    def greet(i, _):
+        other = lax.rem(chip + i, chips) * 2 + core
+        pl.semaphore_signal(barrier, inc=1, device_id=(other, y), device_id_type=MESH)
+        return 0
+
+    lax.fori_loop(1, chips, greet, 0)
+
     w_loads = [
         pltpu.make_async_copy(
             w_hbm.at[:, pl.ds(pl.multiple_of(column(b, side, y), block), block)], w_own.at[b], w_sem.at[b])
@@ -162,11 +169,8 @@
                 spread(f, path, i // 3, i % 3 + 1, False).wait_send()
         share(f, core).wait_send()
 
-    pl.semaphore_wait(barrier, chips + 2)
-    gather(0, 0)
-    gather(1, 0)
-    for c in w_loads:
-        c.start()
+    for c in gates:
+        c.wait()
     cum = running(log_sigmoid(stacked(gate_f[...])), jnp.add, 0.0)
     g = stacked(gate_in[...]) - cum
     peak = running(g, jnp.maximum, LOW)
@@ -175,6 +179,9 @@
     g, peak = unstacked(g), unstacked(peak)
     grow[0:2, :] = g
     gcol[...] = jnp.transpose(jnp.concatenate([g, peak, g, peak], axis=0), (1, 0))
+    pl.semaphore_wait(barrier, chips + 2)
+    gather(0, 0)
+    gather(1, 0)
     for c in (0, 1, 3, 4):
         loads[c].wait()
     swap = [
@@ -288,6 +295,8 @@
 
     for f in range(2, 5):
         gather(f, 0)
+    for c in w_loads:
+        c.start()
     attend(0)
     gather(1, 1)
     gather(0, 2)
@@ -351,6 +360,7 @@
 
     gather(0, 3)
     gather(1, 2)
+    gather(3, 1)
     pm, pn = pre_n[2:3, :], pre_n[0:2, :]
     top = jnp.maximum(pm + f0, t0)
     a, b = jnp.exp(pm + f0 - top), jnp.exp(t0 - top)
@@ -378,36 +388,45 @@
     ]
     for c in tell:
         c.start()
+
+    def finish_head(start, size, h):
+        at = pl.ds(pl.multiple_of(start, 32), size)
+        pm = fix_n[h, 2:3, 0:1]
+        n_row = jnp.concatenate([fix_n[h, 0:1, :], fix_n[h, 1:2, :]], axis=1)
+        peak_col = jnp.where(h == 0, gcol[at, 2:3], gcol[at, 3:4])
+        top = jnp.maximum(peak_col, pm)
+        ow, iw = jnp.exp(peak_col - top), jnp.exp(pm - top)
+        mem = jnp.dot(qc[h, at, 0:256], fix[h], preferred_element_type=F32)
+        mem_n = jnp.sum(qf[h, at, :] * n_row, axis=1, keepdims=True)
+        d = jnp.maximum(jnp.abs(ow * den[h, at, :] + iw * mem_n), 1.0)
+        inv = 1.0 / d
+        hidden[at, pl.ds(pl.multiple_of(h * width, width), width)] = (
+            (ow * inv) * num[h, at, :] + (iw * inv) * mem
+        ).astype(BF16)
+
+    def finish(start, size):
+        finish_head(start, size, 1 - core)
+
+    def ready_head(i, _):
+        finish_head(i * tile, tile, core)
+        return 0
+
+    lax.fori_loop(0, rows // tile, ready_head, 0)
     for c in tell:
         c.wait()
 
-    def finish(start, count):
-        at = pl.ds(pl.multiple_of(start, 64), count)
-        for h in range(2):
-            pm = fix_n[h, 2:3, 0:1]
-            n_row = jnp.concatenate([fix_n[h, 0:1, :], fix_n[h, 1:2, :]], axis=1)
-            peak_col = gcol[at, 2 + h:3 + h]
-            top = jnp.maximum(peak_col, pm)
-            ow, iw = jnp.exp(peak_col - top), jnp.exp(pm - top)
-            mem = jnp.dot(qc[h, at, 0:256], fix[h], preferred_element_type=F32)
-            mem_n = jnp.sum(qf[h, at, :] * n_row, axis=1, keepdims=True)
-            d = jnp.maximum(jnp.abs(ow * den[h, at, :] + iw * mem_n), 1.0)
-            inv = 1.0 / d
-            hidden[at, h * width:(h + 1) * width] = (
-                (ow * inv) * num[h, at, :] + (iw * inv) * mem
-            ).astype(BF16)
-
-    small, count = 64, 4
-    big = half - small * count
+
+    edge, small, count = 32, 64, 4
+    big = half - edge - small * count
 
     def rows_at(mine, c):
-        base = (kept if mine else 1 - kept) * half
+        base = (kept if mine else 1 - kept) * half + edge
         return base + c * small, (small if c is not count else big)
 
     def x_copy(c):
         start, size = rows_at(False, c)
         return pltpu.make_async_remote_copy(
-            src_ref=hidden.at[pl.ds(pl.multiple_of(start, small), size)],
+            src_ref=hidden.at[pl.ds(pl.multiple_of(start, edge), size)],
             dst_ref=swapped.at[pl.ds(pl.multiple_of(c * small, small), size)], send_sem=xs.at[c], recv_sem=xr.at[c],
             device_id=(ctx, partner), device_id_type=MESH)
 
@@ -431,14 +450,14 @@
         start, size = rows_at(not incoming, c)
         return pltpu.make_async_remote_copy(
             src_ref=z_out.at[pl.ds(pl.multiple_of(c * small, small), size), pl.ds(lo, w)],
-            dst_ref=out.at[pl.ds(pl.multiple_of(start, small), size), pl.ds(lo, w)],
+            dst_ref=out.at[pl.ds(pl.multiple_of(start, edge), size), pl.ds(lo, w)],
             send_sem=zs.at[i], recv_sem=zr.at[i], device_id=(ctx, partner), device_id_type=MESH)
 
     def project(f, piece):
         c, b, lo, w, i = piece
         start, size = rows_at(True, c)
         return jnp.dot(
-            hidden[pl.ds(pl.multiple_of(start, small), size), :], w_own[f, :, pl.ds(lo, w)],
+            hidden[pl.ds(pl.multiple_of(start, edge), size), :], w_own[f, :, pl.ds(lo, w)],
             preferred_element_type=F32,
         ) + jnp.dot(
             swapped[pl.ds(pl.multiple_of(c * small, small), size), :], w_mate[f, :, pl.ds(lo, w)],
@@ -449,6 +468,13 @@
         c, b, lo, w, i = piece
         y_out[b, pl.ds(pl.multiple_of(c * small, small), rows_at(True, c)[1]), pl.ds(lo, w)] = project(b, piece).astype(BF16)
         y_copy(piece).start()
+
+    def keep(piece):
+        c, b, lo, w, i = piece
+        start, size = rows_at(True, c)
+        return pltpu.make_async_copy(
+            out_own.at[pl.ds(pl.multiple_of(c * small, small), size), pl.ds(lo, w)],
+            out.at[pl.ds(pl.multiple_of(start, edge), size), pl.ds(lo, w)], own_sem.at[i])
 
     def f_step(piece):
         c, b, lo, w, i = piece
@@ -461,7 +487,8 @@
             z_out[at, pl.ds(lo, w)] = total
             z_copy(piece, False).start()
         else:
-            out[pl.ds(pl.multiple_of(start, small), size), pl.ds(lo, w)] = total
+            out_own[at, pl.ds(lo, w)] = total
+            keep(piece).start()
 
     def each(n, body):
         def one(i, _):
@@ -475,16 +502,41 @@
         if not mine:
             x_copy(c).start()
 
+    ends = (0, half)
+
+    def edge_rows():
+        return jnp.concatenate([hidden[pl.ds(e, edge), :] for e in ends], axis=0)
+
+    def edge_copy(b):
+        return pltpu.make_async_remote_copy(
+            src_ref=e_out.at[b], dst_ref=e_in.at[b], send_sem=edge_s.at[b], recv_sem=edge_r.at[b],
+            device_id=(ctx, across), device_id_type=MESH)
+
+    def edge_sum():
+        return pltpu.make_async_remote_copy(
+            src_ref=e_sum, dst_ref=e_got, send_sem=edge_s.at[2], recv_sem=edge_r.at[2],
+            device_id=(ctx, partner), device_id_type=MESH)
+
+    def edge_keep(i):
+        return pltpu.make_async_copy(
+            e_sum2.at[pl.ds(i * edge, edge)], out.at[pl.ds(ends[i], edge)], edge_k.at[i])
+
     finish_chunk(False, 0)
+    for e in ends:
+        finish(e, edge)
+    for b in range(2):
+        w_loads[b].wait()
+        e_out[b] = jnp.dot(edge_rows(), w_own[b], preferred_element_type=F32).astype(BF16)
+        edge_copy(b).start()
     finish_chunk(True, 0)
     each(count - 1, lambda i: finish_chunk(False, i + 1))
     gather(2, 2)
-    gather(3, 1)
+    gather(4, 1)
     finish_chunk(False, count)
     each(count - 1, lambda i: finish_chunk(True, i + 1))
     finish_chunk(True, count)
-    for c in w_loads:
-        c.wait()
+    w_loads[2].wait()
+    w_loads[3].wait()
     gather(1, 3)
     gather(0, 4)
 
@@ -495,23 +547,23 @@
         @pl.when(c == 0)
         def _():
             gather(1, 4)
+            gather(3, 2)
 
         y_step(small_piece(c, 1))
-
-        @pl.when(c == 1)
-        def _():
-            gather(3, 2)
-            gather(4, 1)
 
         @pl.when(c == 2)
         def _():
             gather(2, 3)
+            gather(4, 2)
 
     each(count, first_columns)
+    edge_copy(0).wait_recv()
+    e_sum[...] = (
+        jnp.dot(edge_rows(), w_own[2], preferred_element_type=F32) + e_in[0].astype(F32)).astype(BF16)
+    edge_sum().start()
     gather(2, 4)
     each(count, lambda c: y_step(small_piece(c, 2)))
     gather(3, 3)
-    gather(4, 2)
     gather(3, 4)
 
     def for_partner(c):
@@ -519,6 +571,12 @@
         f_step(small_piece(c, 1))
 
     each(count, for_partner)
+    edge_copy(1).wait_recv()
+    own_edge = jnp.dot(edge_rows(), w_own[3], preferred_element_type=F32) + e_in[1].astype(F32)
+    edge_sum().wait_recv()
+    e_sum2[...] = (own_edge + e_got[...].astype(F32)).astype(BF16)
+    for i in range(2):
+        edge_keep(i).start()
     x_copy(count).wait_recv()
     each(4, lambda j: y_step(big_piece(0, j)))
     each(4, lambda j: y_step(big_piece(1, j)))
@@ -530,9 +588,14 @@
 
     for f in range(5):
         gather_sent(f)
+    edge_sum().wait_send()
+    for i in range(2):
+        edge_copy(i).wait_send()
+        edge_keep(i).wait()
 
     def small_done(c):
         x_copy(c).wait_send()
+        keep(small_piece(c, 2)).wait()
         for p in range(3):
             y_copy(small_piece(c, p)).wait_send()
         for p in range(2):
@@ -542,6 +605,7 @@
     def big_done(j):
         y_copy(big_piece(0, j)).wait_send()
         y_copy(big_piece(1, j)).wait_send()
+        keep(big_piece(1, j)).wait()
         z_copy(big_piece(0, j), False).wait_send()
         z_copy(big_piece(0, j), True).wait_recv()
 
@@ -565,15 +629,15 @@
     chips = lax.axis_size("ctx") // 2
     part = dk // chips
     hbm = pl.BlockSpec(memory_space=pl.ANY)
-    vmem = pl.BlockSpec(memory_space=pltpu.VMEM)
     V = pltpu.VMEM
     dma = pltpu.SemaphoreType.DMA
     return pl.pallas_call(
         layer_kernel,
         out_shape=jax.ShapeDtypeStruct((rows, out_weight.shape[1] // 4), BF16),
-        in_specs=[hbm, hbm, hbm, hbm, vmem, vmem],
-        out_specs=vmem,
+        in_specs=[hbm] * 6,
+        out_specs=hbm,
         scratch_shapes=[
+            V((heads, rows), F32), V((heads, rows), F32),
             V((heads, rows, dk), F32), V((heads, rows, dk), F32), V((heads, rows, dv), F32),
             V((heads, rows, 3 * dk), BF16), V((rows, 3 * dk), BF16), V((heads, rows, dv), BF16),
             V((heads, rows, dv), F32), V((heads, rows, 1), F32), V((rows, 8), F32), V((8, rows), F32),
@@ -586,7 +650,10 @@
             V((4, heads * dv, out_weight.shape[1] // 4), BF16), V((4, heads * dv, out_weight.shape[1] // 4), BF16),
             V((2, rows // 2, out_weight.shape[1] // 4), BF16), V((2, rows // 2, out_weight.shape[1] // 4), BF16),
             V((rows // 2, out_weight.shape[1] // 4), BF16),
-            dma((2, 3)), dma((4,)), dma((8,)), dma((chips,)), dma((chips,)), dma((chips,)), dma((chips,)),
+            V((2, 64, out_weight.shape[1] // 4), BF16), V((2, 64, out_weight.shape[1] // 4), BF16),
+            V((64, out_weight.shape[1] // 4), BF16), V((64, out_weight.shape[1] // 4), BF16),
+            V((64, out_weight.shape[1] // 4), BF16), dma((3,)), dma((3,)), dma((2,)),
+            V((rows // 2, out_weight.shape[1] // 4), BF16), dma((2,)), dma((20,)), dma((2, 3)), dma((4,)), dma((8,)), dma((chips,)), dma((chips,)), dma((chips,)), dma((chips,)),
             dma((chips,)), dma((chips,)),
             dma((5, 2)), dma((5, 2)), dma((5, 2, 6)), dma((5, 2, 6)), dma((5,)), dma((5,)),
             dma((5,)), dma((5,)), dma((20,)), dma((20,)), dma((20,)), dma((20,)),
@@ -598,8 +665,35 @@
     )(queries, keys, values, out_weight, gate_in, gate_f)
 
 
+def hand_kernel(src, dst, held, in_sem, out_sem):
+    count = in_sem.shape[0]
+    size = src.shape[0] // count
+    at = [pl.ds(i * size, size) for i in range(count)]
+    take = [pltpu.make_async_copy(src.at[a], held.at[a], in_sem.at[i]) for i, a in enumerate(at)]
+    give = [pltpu.make_async_copy(held.at[a], dst.at[a], out_sem.at[i]) for i, a in enumerate(at)]
+    for c in take:
+        c.start()
+    for c, d in zip(take, give):
+        c.wait()
+        d.start()
+    for d in give:
+        d.wait()
+
+
+def handed_on(x):
+    hbm = pl.BlockSpec(memory_space=pl.ANY)
+    return pl.pallas_call(
+        hand_kernel,
+        out_shape=jax.ShapeDtypeStruct(x.shape, x.dtype),
+        in_specs=[hbm],
+        out_specs=hbm,
+        scratch_shapes=[pltpu.VMEM(x.shape, x.dtype), pltpu.SemaphoreType.DMA((8,)), pltpu.SemaphoreType.DMA((8,))],
+        name="hand_on",
+    )(x)
+
+
 def on_device(queries, keys, values, entry_gate_logit, forget_gate, out_weight):
-    return layer(queries, keys, values, out_weight, entry_gate_logit, forget_gate)
+    return handed_on(layer(queries, keys, values, out_weight, entry_gate_logit, forget_gate))
 
 
 def solution(mesh):

time: 91.4 us -> 84.7 us (0.927)
  Pallas kernels: 88.1 us -> 84.6 us
  local copies, waits for them, and re-layouts: 3.08 us -> 0 us
    pallas_call x1, Pallas kernels: 88.1 us -> 82.2 us  [layer(): pl.pallas_call(layer_kernel, out_shape=jax.ShapeDtypeStruct((rows, out_we...]
    unnamed x1 -> x0, local copies, waits for them, and re-layouts: 3.08 us -> none
    pallas_call x0 -> x1, Pallas kernels: none -> 2.39 us  [handed_on(): pl.pallas_call(hand_kernel, out_shape=jax.ShapeDtypeStruct(x.shape, x.dty...]
where the time goes in v4:
time: 84.7 us; the launch traced here: 84.6 us
  Pallas kernels  84.6 us (100%)
    pallas_call x1, Pallas kernels, layer(): pl.pallas_call(layer_kernel, out_shape=jax.ShapeDtypeStruct((rows, out_we...  82.2 us
    pallas_call x1, Pallas kernels, handed_on(): pl.pallas_call(hand_kernel, out_shape=jax.ShapeDtypeStruct(x.shape, x.dty...  2.39 us

profile of v4, /device:TPU:1, one launch (start us, length us, event | category | flops | bytes accessed | tf_op | source)
XLA Modules:
  0.0 84.6 jit_solution(16424016148111535093)
XLA Ops:
  0.0 82.2 %layer.1.src = bf16[1024,1024]{1,0:T(8,128)(2,1)} custom-call(f32[1024,2,256]{2,1,0:T(2,128)} %q_hbm.1, f32[1024,2,256]{2,1,0:T(2,128)} %k_hbm.1, f32[1024,2,512]{2,1,0:T(2,128)} %v_hbm.1, bf16[1024,4096]{1,0:T(8,128)(2,1)} %w_hbm.1, f32[2,1024]{1,0:T(2,128)} %in_hbm.1, f32[2,1024]{1,0:T(2,128)} %f_hbm.1), custom_call_target="tpu_custom_call" | custom-call | tf_op jit(solution)/shard_map/layer/pallas_call | solution.py:634
  82.2 2.4 %hand_on.1 = bf16[1024,1024]{1,0:T(8,128)(2,1)} custom-call(bf16[1024,1024]{1,0:T(8,128)(2,1)} %layer.1.src), custom_call_target="tpu_custom_call" | custom-call | tf_op jit(solution)/shard_map/hand_on/pallas_call | solution.py:685

commit v5 on v4

--- a/solution.py
+++ b/solution.py
@@ -49,7 +49,7 @@
     qf, kf, vf, qc, kc, vb, num, den, gcol, grow, own_c, own_n, gone, gone_n, came, came_n,
     chip_c, chip_n, slots, slots_n, back, prefix, pre_n, fix, fix_n, out_c, out_n,
     hidden, swapped, w_own, w_mate, y_out, y_in, z_out,
-    e_out, e_in, e_sum, e_got, e_sum2, edge_s, edge_r, edge_k, out_own, gate_sem, own_sem, load_sem, w_sem, pair_sem, ss, rs, sns, rns, sb, rb,
+    weigh, e_out, e_in, e_sum, e_got, e_sum2, edge_s, edge_r, edge_k, out_own, gate_sem, own_sem, load_sem, w_sem, pair_sem, ss, rs, sns, rns, sb, rb,
     fetch_s, fetch_r, ring_s, ring_r, share_s, share_r, xs, xr, ys, yr, zs, zr,
 ):
     rows = q_hbm.shape[0]
@@ -74,6 +74,14 @@
         start = (lax.div(of_y, 2) * -2 + 2 + part_of, lax.div(of_y, 2) * -2 + 3 - part_of, other, of_y)[b]
         return start * block
 
+    barrier = pltpu.get_barrier_semaphore()
+    for who in ((mate, y), (ctx, partner), (ctx, across)):
+        pl.semaphore_signal(barrier, inc=1, device_id=who, device_id_type=MESH)
+
+    for i in range(1, chips):
+        other = lax.rem(chip + i, chips) * 2 + core
+        pl.semaphore_signal(barrier, inc=1, device_id=(other, y), device_id_type=MESH)
+
     gates = [
         pltpu.make_async_copy(f_hbm, gate_f, gate_sem.at[0]),
         pltpu.make_async_copy(in_hbm, gate_in, gate_sem.at[1]),
@@ -86,17 +94,6 @@
             loads.append(pltpu.make_async_copy(src.at[:, h, :], dst.at[h], load_sem.at[h, j]))
     for c in (0, 1, 3, 4, 2, 5):
         loads[c].start()
-    barrier = pltpu.get_barrier_semaphore()
-    for who in ((mate, y), (ctx, partner), (ctx, across)):
-        pl.semaphore_signal(barrier, inc=1, device_id=who, device_id_type=MESH)
-
-    def greet(i, _):
-        other = lax.rem(chip + i, chips) * 2 + core
-        pl.semaphore_signal(barrier, inc=1, device_id=(other, y), device_id_type=MESH)
-        return 0
-
-    lax.fori_loop(1, chips, greet, 0)
-
     w_loads = [
         pltpu.make_async_copy(
             w_hbm.at[:, pl.ds(pl.multiple_of(column(b, side, y), block), block)], w_own.at[b], w_sem.at[b])
@@ -179,9 +176,6 @@
     g, peak = unstacked(g), unstacked(peak)
     grow[0:2, :] = g
     gcol[...] = jnp.transpose(jnp.concatenate([g, peak, g, peak], axis=0), (1, 0))
-    pl.semaphore_wait(barrier, chips + 2)
-    gather(0, 0)
-    gather(1, 0)
     for c in (0, 1, 3, 4):
         loads[c].wait()
     swap = [
@@ -209,11 +203,13 @@
         own_n[h, 3:4, :] = jnp.broadcast_to(top + end, (1, 128))
         if turn == 0:
             gone[...] = state.astype(BF16)
+            pl.semaphore_wait(barrier, chips + 2)
             for c in swap:
                 c.start()
+            gather(0, 0)
+            gather(1, 0)
         else:
             own_c[...] = state
-    gather(0, 1)
     for c in swap:
         c.wait()
 
@@ -261,6 +257,7 @@
         return 0
 
     lax.fori_loop(1, chips, send, 0)
+    gather(0, 1)
     slots_n[chip] = chip_n[...]
     slots[chip] = chip_c[pl.ds(pl.multiple_of(chip * part, part), part), :]
 
@@ -299,19 +296,6 @@
         c.start()
     attend(0)
     gather(1, 1)
-    gather(0, 2)
-
-    def got_n(i, _):
-        from_chip(lax.rem(chip + i, chips))[0].wait_recv()
-        return 0
-
-    lax.fori_loop(1, chips, got_n, 0)
-
-    def got_c(i, _):
-        from_chip(lax.rem(chip + i, chips))[1].wait_recv()
-        return 0
-
-    lax.fori_loop(1, chips, got_c, 0)
 
     def give_back(other):
         return pltpu.make_async_remote_copy(
@@ -323,31 +307,46 @@
             src_ref=back.at[other], dst_ref=prefix.at[pl.ds(pl.multiple_of(other * part, part), part)],
             send_sem=sb.at[other], recv_sem=rb.at[other], device_id=(other * 2 + core, y), device_id_type=MESH)
 
-    def scan(p, carry):
-        m, c, n = carry
-        back[p] = c.astype(BF16)
+    def factors(p, carry):
+        m, n = carry
+
+        @pl.when(p != chip)
+        def _():
+            from_chip(p)[0].wait_recv()
 
         @pl.when(p == chip)
         def _():
             pre_n[0:2, :] = n
             pre_n[2:3, :] = m
-            prefix[pl.ds(pl.multiple_of(chip * part, part), part), :] = c.astype(BF16)
-
-        @pl.when(p != chip)
-        def _():
-            give_back(p).start()
 
         later = slots_n[p]
         f, t = later[2:3], later[3:4]
         top = jnp.maximum(m + f, t)
         a, b = jnp.exp(m + f - top), jnp.exp(t - top)
-        c = c * wide(a, width) + slots[p].astype(F32) * wide(b, width)
-        return top, c, n * a + later[0:2] * b
-
-    lax.fori_loop(
-        0, chips, scan,
-        (jnp.full((1, 128), LOW, F32), jnp.zeros((part, width), F32), jnp.zeros((2, 128), F32)),
-    )
+        weigh[p, 0:1, :] = a
+        weigh[p, 1:2, :] = b
+        return top, n * a + later[0:2] * b
+
+    lax.fori_loop(0, chips, factors, (jnp.full((1, 128), LOW, F32), jnp.zeros((2, 128), F32)))
+
+    def scan(p, c):
+        @pl.when(p != chip)
+        def _():
+            from_chip(p)[1].wait_recv()
+
+        back[p] = c.astype(BF16)
+
+        @pl.when(p == chip)
+        def _():
+            prefix[pl.ds(pl.multiple_of(chip * part, part), part), :] = c.astype(BF16)
+
+        @pl.when(p != chip)
+        def _():
+            give_back(p).start()
+
+        return c * wide(weigh[p, 0:1, :], width) + slots[p].astype(F32) * wide(weigh[p, 1:2, :], width)
+
+    lax.fori_loop(0, chips, scan, jnp.zeros((part, width), F32))
 
     attend(1)
     gather(2, 1)
@@ -358,9 +357,7 @@
 
     lax.fori_loop(1, chips, got_back, 0)
 
-    gather(0, 3)
-    gather(1, 2)
-    gather(3, 1)
+    gather(0, 2)
     pm, pn = pre_n[2:3, :], pre_n[0:2, :]
     top = jnp.maximum(pm + f0, t0)
     a, b = jnp.exp(pm + f0 - top), jnp.exp(t0 - top)
@@ -412,6 +409,8 @@
         return 0
 
     lax.fori_loop(0, rows // tile, ready_head, 0)
+    gather(1, 2)
+    gather(3, 1)
     for c in tell:
         c.wait()
 
@@ -530,9 +529,10 @@
         edge_copy(b).start()
     finish_chunk(True, 0)
     each(count - 1, lambda i: finish_chunk(False, i + 1))
+    finish_chunk(False, count)
+    gather(0, 3)
     gather(2, 2)
     gather(4, 1)
-    finish_chunk(False, count)
     each(count - 1, lambda i: finish_chunk(True, i + 1))
     finish_chunk(True, count)
     w_loads[2].wait()
@@ -650,6 +650,7 @@
             V((4, heads * dv, out_weight.shape[1] // 4), BF16), V((4, heads * dv, out_weight.shape[1] // 4), BF16),
             V((2, rows // 2, out_weight.shape[1] // 4), BF16), V((2, rows // 2, out_weight.shape[1] // 4), BF16),
             V((rows // 2, out_weight.shape[1] // 4), BF16),
+            V((chips, 2, 128), F32),
             V((2, 64, out_weight.shape[1] // 4), BF16), V((2, 64, out_weight.shape[1] // 4), BF16),
             V((64, out_weight.shape[1] // 4), BF16), V((64, out_weight.shape[1] // 4), BF16),
             V((64, out_weight.shape[1] // 4), BF16), dma((3,)), dma((3,)), dma((2,)),

time: 84.7 us -> 83.4 us (0.985)
  Pallas kernels: 84.6 us -> 83.2 us
    pallas_call x1, Pallas kernels: 82.2 us -> 80.8 us  [layer(): pl.pallas_call(layer_kernel, out_shape=jax.ShapeDtypeStruct((rows, out_we...]
where the time goes in v5:
time: 83.4 us; the launch traced here: 83.2 us
  Pallas kernels  83.2 us (100%)
    pallas_call x1, Pallas kernels, layer(): pl.pallas_call(layer_kernel, out_shape=jax.ShapeDtypeStruct((rows, out_we...  80.8 us
    pallas_call x1, Pallas kernels, handed_on(): pl.pallas_call(hand_kernel, out_shape=jax.ShapeDtypeStruct(x.shape, x.dty...  2.39 us

profile of v5, /device:TPU:1, one launch (start us, length us, event | category | flops | bytes accessed | tf_op | source)
XLA Modules:
  0.0 83.2 jit_solution(6352921292024313453)
XLA Ops:
  0.0 80.8 %layer.1.src = bf16[1024,1024]{1,0:T(8,128)(2,1)} custom-call(f32[1024,2,256]{2,1,0:T(2,128)} %q_hbm.1, f32[1024,2,256]{2,1,0:T(2,128)} %k_hbm.1, f32[1024,2,512]{2,1,0:T(2,128)} %v_hbm.1, bf16[1024,4096]{1,0:T(8,128)(2,1)} %w_hbm.1, f32[2,1024]{1,0:T(2,128)} %in_hbm.1, f32[2,1024]{1,0:T(2,128)} %f_hbm.1), custom_call_target="tpu_custom_call" | custom-call | tf_op jit(solution)/shard_map/layer/pallas_call | solution.py:634
  80.9 2.4 %hand_on.1 = bf16[1024,1024]{1,0:T(8,128)(2,1)} custom-call(bf16[1024,1024]{1,0:T(8,128)(2,1)} %layer.1.src), custom_call_target="tpu_custom_call" | custom-call | tf_op jit(solution)/shard_map/hand_on/pallas_call | solution.py:686

commit v6 on v5

--- a/solution.py
+++ b/solution.py
@@ -49,7 +49,7 @@
     qf, kf, vf, qc, kc, vb, num, den, gcol, grow, own_c, own_n, gone, gone_n, came, came_n,
     chip_c, chip_n, slots, slots_n, back, prefix, pre_n, fix, fix_n, out_c, out_n,
     hidden, swapped, w_own, w_mate, y_out, y_in, z_out,
-    weigh, e_out, e_in, e_sum, e_got, e_sum2, edge_s, edge_r, edge_k, out_own, gate_sem, own_sem, load_sem, w_sem, pair_sem, ss, rs, sns, rns, sb, rb,
+    plane_sem, weigh, e_out, e_in, e_sum, e_got, e_sum2, edge_s, edge_r, edge_k, out_own, gate_sem, own_sem, load_sem, w_sem, pair_sem, ss, rs, sns, rns, sb, rb,
     fetch_s, fetch_r, ring_s, ring_r, share_s, share_r, xs, xr, ys, yr, zs, zr,
 ):
     rows = q_hbm.shape[0]
@@ -78,8 +78,9 @@
     for who in ((mate, y), (ctx, partner), (ctx, across)):
         pl.semaphore_signal(barrier, inc=1, device_id=who, device_id_type=MESH)
 
-    for i in range(1, chips):
-        other = lax.rem(chip + i, chips) * 2 + core
+    x_line = [(cz * 4 + lax.rem(cx + i, 4)) * 2 + core for i in range(1, 4)]
+    z_line = [(lax.rem(cz + i, 4) * 4 + cx) * 2 + core for i in range(1, 4)]
+    for other in x_line + z_line:
         pl.semaphore_signal(barrier, inc=1, device_id=(other, y), device_id_type=MESH)
 
     gates = [
@@ -203,7 +204,9 @@
         own_n[h, 3:4, :] = jnp.broadcast_to(top + end, (1, 128))
         if turn == 0:
             gone[...] = state.astype(BF16)
-            pl.semaphore_wait(barrier, chips + 2)
+            pl.semaphore_wait(barrier, 9)
+            for other in z_line:
+                pl.semaphore_signal(plane_sem, inc=1, device_id=(other, y), device_id_type=MESH)
             for c in swap:
                 c.start()
             gather(0, 0)
@@ -256,6 +259,7 @@
             c.start()
         return 0
 
+    pl.semaphore_wait(plane_sem, 3)
     lax.fori_loop(1, chips, send, 0)
     gather(0, 1)
     slots_n[chip] = chip_n[...]
@@ -650,7 +654,7 @@
             V((4, heads * dv, out_weight.shape[1] // 4), BF16), V((4, heads * dv, out_weight.shape[1] // 4), BF16),
             V((2, rows // 2, out_weight.shape[1] // 4), BF16), V((2, rows // 2, out_weight.shape[1] // 4), BF16),
             V((rows // 2, out_weight.shape[1] // 4), BF16),
-            V((chips, 2, 128), F32),
+            pltpu.SemaphoreType.REGULAR, V((chips, 2, 128), F32),
             V((2, 64, out_weight.shape[1] // 4), BF16), V((2, 64, out_weight.shape[1] // 4), BF16),
             V((64, out_weight.shape[1] // 4), BF16), V((64, out_weight.shape[1] // 4), BF16),
             V((64, out_weight.shape[1] // 4), BF16), dma((3,)), dma((3,)), dma((2,)),
@@ -688,7 +692,7 @@
         out_shape=jax.ShapeDtypeStruct(x.shape, x.dtype),
         in_specs=[hbm],
         out_specs=hbm,
-        scratch_shapes=[pltpu.VMEM(x.shape, x.dtype), pltpu.SemaphoreType.DMA((8,)), pltpu.SemaphoreType.DMA((8,))],
+        scratch_shapes=[pltpu.VMEM(x.shape, x.dtype), pltpu.SemaphoreType.DMA((4,)), pltpu.SemaphoreType.DMA((4,))],
         name="hand_on",
     )(x)
 

time: 83.4 us -> 83.1 us (level)
  no operation moved by 1% of the time
where the time goes in v6:
time: 83.1 us; the launch traced here: 83 us
  Pallas kernels  83 us (100%)
    pallas_call x1, Pallas kernels, layer(): pl.pallas_call(layer_kernel, out_shape=jax.ShapeDtypeStruct((rows, out_we...  80.5 us
    pallas_call x1, Pallas kernels, handed_on(): pl.pallas_call(hand_kernel, out_shape=jax.ShapeDtypeStruct(x.shape, x.dty...  2.42 us

profile of v6, /device:TPU:1, one launch (start us, length us, event | category | flops | bytes accessed | tf_op | source)
XLA Modules:
  0.0 83.0 jit_solution(14189483458849687905)
XLA Ops:
  0.0 80.5 %layer.1.src = bf16[1024,1024]{1,0:T(8,128)(2,1)} custom-call(f32[1024,2,256]{2,1,0:T(2,128)} %q_hbm.1, f32[1024,2,256]{2,1,0:T(2,128)} %k_hbm.1, f32[1024,2,512]{2,1,0:T(2,128)} %v_hbm.1, bf16[1024,4096]{1,0:T(8,128)(2,1)} %w_hbm.1, f32[2,1024]{1,0:T(2,128)} %in_hbm.1, f32[2,1024]{1,0:T(2,128)} %f_hbm.1), custom_call_target="tpu_custom_call" | custom-call | tf_op jit(solution)/shard_map/layer/pallas_call | solution.py:638
  80.5 2.4 %hand_on.1 = bf16[1024,1024]{1,0:T(8,128)(2,1)} custom-call(bf16[1024,1024]{1,0:T(8,128)(2,1)} %layer.1.src), custom_call_target="tpu_custom_call" | custom-call | tf_op jit(solution)/shard_map/hand_on/pallas_call | solution.py:690
